TPU v7x, 512 devices: a whole 4x8x8 slice. The times are simulated.
512 devices in a mesh: dp: 32 (over y, z_lo, core), mp: 16 (over x, z_hi).
Axes of the slice: x: 4, y: 8, z: 8 (z_hi: 4, z_lo: 2; z = z_hi * 2 + z_lo), core: 2. Of those that a mesh axis runs over, the one named last changes fastest.
Arguments:
- tokens: bfloat16 [4096, 8192], P(('dp', 'mp')), may hold values from -6 to 6
- kv_weight: bfloat16 [8192, 2048], P(None, 'mp'), may hold values from -0.125 to 0.125
- out_grad: bfloat16 [4096, 2048], P('dp', 'mp'), may hold values from -6 to 6
- basis: bfloat16 [8192, 1024], P(None, 'mp'), may hold values from -0.0625 to 0.0625
- first_moment: float32 [1024, 2048], P('mp', 'dp'), may hold values from -96 to 96
- second_moment: float32 [1024, 2048], P('mp', 'dp'), may hold values from 8 to 200
Outputs:
- input_grad: bfloat16 [4096, 8192], P(('dp', 'mp'))
- update: bfloat16 [8192, 2048], P('mp', 'dp')
- new_first: float32 [1024, 2048], P('mp', 'dp')
- new_second: float32 [1024, 2048], P('mp', 'dp')
All inputs are finite; a program needn't handle non-finite values.
Results may differ from a plain program's by a relative error of at most 0.023.
Values may be sent and summed in bfloat16 or wider, within the bound.
No kernel may reach another device: no remote copies, remote signals or barrier semaphores. Data moves between devices by JAX's collectives and lax.ppermute only.
A program may use at most 64 MiB of HBM per device.

v0:
```python
import jax
import jax.numpy as jnp
from jax import lax
from jax.sharding import PartitionSpec as P

STEP = 10


epsilon = 1e-08


def body(tokens, kv_weight, out_grad, basis, first_moment, second_moment):
    projected = jnp.dot(
        lax.all_gather(tokens, "mp", axis=0, tiled=True), basis, preferred_element_type=jnp.float32
    ).astype(jnp.bfloat16)
    grad_all = lax.all_gather(out_grad, "mp", axis=1, tiled=True)
    partial_grad = jnp.dot(projected.T, grad_all, preferred_element_type=jnp.float32)
    col_width = first_moment.shape[1]
    summed_all = lax.psum(partial_grad.astype(jnp.bfloat16), "dp").astype(jnp.float32)
    local_grad = lax.dynamic_slice_in_dim(
        summed_all, lax.axis_index("dp") * col_width, col_width, 1
    )
    new_first = 0.9 * first_moment + 0.1 * local_grad
    new_second = 0.999 * second_moment + 0.001 * local_grad * local_grad
    first_scale = 1.0 - 0.9**STEP
    second_scale = 1.0 - 0.999**STEP
    direction = (new_first / first_scale / (jnp.sqrt(new_second / second_scale) + epsilon)).astype(
        jnp.bfloat16
    )
    update = lax.psum_scatter(
        jnp.dot(basis, direction, preferred_element_type=jnp.float32).astype(jnp.bfloat16),
        "mp",
        scatter_dimension=0,
        tiled=True,
    )
    input_grad = lax.psum_scatter(
        lax.dot_general(
            out_grad, kv_weight, (((1,), (1,)), ((), ())), preferred_element_type=jnp.float32
        ).astype(jnp.bfloat16),
        "mp",
        scatter_dimension=0,
        tiled=True,
    )
    return (input_grad, update, new_first, new_second)


def solution(mesh):
    placed = (
        P(("dp", "mp"), None),
        P(None, "mp"),
        P("dp", "mp"),
        P(None, "mp"),
        P("mp", "dp"),
        P("mp", "dp"),
    )
    return jax.shard_map(
        body,
        mesh=mesh,
        in_specs=placed,
        out_specs=(P(("dp", "mp"), None), P("mp", "dp"), P("mp", "dp"), P("mp", "dp")),
        check_vma=False,
    )
```

profile of v0, /device:TPU:1, one launch (start us, length us, event | category | flops | bytes accessed | tf_op | source)
XLA Modules:
  0.0 511.6 jit_solution(11320836902301763859)
XLA Ops:
  7.2 0.0 copy-start
  7.2 0.0 all-gather.2.cloned.1.call-start
  7.2 0.7 all-gather.2.cloned.1.call-update
  7.9 0.0 all-reduce.2.cloned.1.call-start
  8.0 46.7 %all_gather.7 = bf16[128,2048]{1,0:T(8,128)(2,1)S(1)} all-gather(bf16[128,128]{1,0:T(8,128)(2,1)} %param.8), channel_id=1, replica_groups=mesh['dp'=32,'mp'=16] {'mp'}, dimensions={1}, use_global_device_ids=true | all-gather | bytes 557056 | tf_op jit(solution)/shard_map/all_gather | solution.py:16
  54.7 0.0 copy-start.2
  54.7 26.4 %all-gather.2.cloned.1.call-done = bf16[128,8192]{1,0:T(8,128)(2,1)} async-done(((bf16[8,8192]{1,0:T(8,128)(2,1)}), bf16[128,8192]{1,0:T(8,128)(2,1)}) %all-gather.2.cloned.1.call-update) | async-done | bytes 2097168 | tf_op jit(solution)/shard_map/all_gather | solution.py:14
  81.1 3.6 convolution_convert_fusion.2
  84.7 0.0 all-reduce.2.cloned.1.call-update
  84.7 0.0 reduce-scatter.3.cloned.1.call-start
  84.8 0.0 copy-done
  84.8 0.0 copy-done.2
  84.8 2.0 convolution_convert_fusion
  86.8 0.0 copy-start.5
  86.8 0.0 copy-start.6
  86.8 0.0 copy-start.1
  86.8 0.0 reduce-scatter.3.cloned.1.call-update
  86.9 0.0 reduce-scatter.5.cloned.1.call-start
  86.9 225.0 %all-reduce.2.cloned.1.call-done = bf16[64,2048]{1,0:T(8,128)(2,1)} async-done(((bf16[64,2048]{1,0:T(8,128)(2,1)}), bf16[64,2048]{1,0:T(8,128)(2,1)}) %all-reduce.2.cloned.1.call-update) | async-done | bytes 262160 | tf_op jit(solution)/shard_map/psum | solution.py:19
  311.9 0.0 copy-done.5
  311.9 0.0 copy-done.6
  311.9 0.8 fusion.1
  312.7 0.0 copy-start.3
  312.7 0.0 copy-start.4
  312.7 0.0 copy-done.1
  312.7 1.5 fusion
  314.2 0.0 reduce-scatter.5.cloned.1.call-update
  314.2 97.3 %reduce-scatter.3.cloned.1.call-done = bf16[8,8192]{1,0:T(8,128)(2,1)} async-done(((bf16[128,8192]{1,0:T(8,128)(2,1)}), bf16[8,8192]{1,0:T(8,128)(2,1)}) %reduce-scatter.3.cloned.1.call-update) | async-done | bytes 131088 | tf_op jit(solution)/shard_map/reduce_scatter | solution.py:36
  411.5 93.5 %reduce-scatter.5.cloned.1.call-done = bf16[512,64]{0,1:T(8,128)(2,1)} async-done(((bf16[8192,64]{0,1:T(8,128)(2,1)}), bf16[512,64]{0,1:T(8,128)(2,1)}) %reduce-scatter.5.cloned.1.call-update) | async-done | bytes 65552 | tf_op jit(solution)/shard_map/reduce_scatter | solution.py:30
  505.0 0.0 copy-done.3
  505.0 0.0 copy-done.4
Async XLA Ops:
  7.2 77.6 %copy-start = (bf16[8192,128]{1,0:T(8,128)(2,1)S(1)}, bf16[8192,128]{1,0:T(8,128)(2,1)}, u32[]{:S(2)}) copy-start(bf16[8192,128]{1,0:T(8,128)(2,1)} %param.7) | copy-start | bytes 6291460
  7.2 73.9 %all-gather.2.cloned.1.call-start = ((), (), s32[]{:S(2)}) async-start(), calls=%async_computation.3 | async-start | bytes 2228224 | tf_op jit(solution)/shard_map/all_gather | solution.py:14
  7.9 304.0 %all-reduce.2.cloned.1.call-start = ((), (), s32[]{:S(2)}) async-start(), calls=%async_computation.4 | async-start | bytes 524288 | tf_op jit(solution)/shard_map/psum | solution.py:19
  54.7 30.1 %copy-start.2 = (bf16[128,128]{1,0:T(8,128)(2,1)S(1)}, bf16[128,128]{1,0:T(8,128)(2,1)}, u32[]{:S(2)}) copy-start(bf16[128,128]{1,0:T(8,128)(2,1)} %param.8) | copy-start | bytes 98308
  84.7 326.8 %reduce-scatter.3.cloned.1.call-start = ((), (), s32[]{:S(2)}) async-start(), calls=%async_computation.2 | async-start | bytes 2228224 | tf_op jit(solution)/shard_map/reduce_scatter | solution.py:36
  86.8 225.1 %copy-start.5 = (f32[64,64]{1,0:T(8,128)S(1)}, f32[64,64]{1,0:T(8,128)}, u32[]{:S(2)}) copy-start(f32[64,64]{1,0:T(8,128)} %param.10) | copy-start | bytes 49156
  86.8 225.1 %copy-start.6 = (f32[64,64]{1,0:T(8,128)S(1)}, f32[64,64]{1,0:T(8,128)}, u32[]{:S(2)}) copy-start(f32[64,64]{1,0:T(8,128)} %param.11) | copy-start | bytes 49156
  86.8 225.9 %copy-start.1 = (bf16[8192,64]{0,1:T(8,128)(2,1)S(1)}, bf16[8192,64]{0,1:T(8,128)(2,1)}, u32[]{:S(2)}) copy-start(bf16[8192,64]{0,1:T(8,128)(2,1)} %param.9) | copy-start | bytes 3145732
  86.9 418.2 %reduce-scatter.5.cloned.1.call-start = ((), (), s32[]{:S(2)}) async-start(), calls=%async_computation.5 | async-start | bytes 1114112 | tf_op jit(solution)/shard_map/reduce_scatter | solution.py:30
  312.7 192.3 %copy-start.3 = (f32[64,64]{1,0:T(8,128)}, f32[64,64]{1,0:T(8,128)S(1)}, u32[]{:S(2)}) copy-start(f32[64,64]{1,0:T(8,128)S(1)} %get-tuple-element.4) | copy-start | bytes 49156
  312.7 192.3 %copy-start.4 = (f32[64,64]{1,0:T(8,128)}, f32[64,64]{1,0:T(8,128)S(1)}, u32[]{:S(2)}) copy-start(f32[64,64]{1,0:T(8,128)S(1)} %get-tuple-element.5) | copy-start | bytes 49156
Sparse Core Ops, SparseCore 0:
  11.0 70.0 all-gather.1
  84.8 226.9 all-reduce.1
  317.2 94.2 reduce-scatter.2
  416.0 88.9 reduce-scatter.4
where the time goes:
time: 513 us; the launch traced here: 512 us
  waiting for transfers between devices  443 us (86%)
  blocking collectives  46.7 us (9%)
  between operations  13.8 us (3%)
  matrix products  7.11 us (1%)
    psum x1, waiting for transfers between devices, body(): lax.psum(partial_grad.astype(jnp.bfloat16), 'dp').astype(jnp.float32)  225 us
    reduce_scatter x1, waiting for transfers between devices, body(): lax.psum_scatter(lax.dot_general(out_grad, kv_weight, (((1,), (1,)), ((),...  97.3 us
    reduce_scatter x1, waiting for transfers between devices, body(): lax.psum_scatter(jnp.dot(basis, direction, preferred_element_type=jnp.flo...  93.5 us
    all_gather x1, blocking collectives, body(): grad_all = lax.all_gather(out_grad, 'mp', axis=1, tiled=True)  46.7 us
    all_gather x1, waiting for transfers between devices, body(): lax.all_gather(tokens, 'mp', axis=0, tiled=True)  26.4 us
  transfers between devices with their start and end apart: 4, of which 4 were waited for; matrix products, arithmetic and copies ran while one was open for 1% of the time, Pallas kernels for 0%

commit v1 on v0

v1 whole, which is shorter than its diff:
```python
import jax
import jax.numpy as jnp
from jax import lax
from jax.sharding import PartitionSpec as P

STEP = 10


epsilon = 1e-08

X, ZH = 4, 4
GROUPS_X = [[z + ZH * x for x in range(X)] for z in range(ZH)]
GROUPS_Z = [[z + ZH * x for z in range(ZH)] for x in range(X)]


def body(tokens, kv_weight, out_grad, basis, first_moment, second_moment):
    n_mp = 16
    rows, width = tokens.shape
    block = width // n_mp
    half = block // 2
    rank = basis.shape[1]
    n_tok = out_grad.shape[0]
    cols = out_grad.shape[1]
    core = lax.axis_index("dp") % 2
    swap = [(d, d ^ 1) for d in range(32)]
    across = [[2 * k + c for k in range(16)] for c in range(2)]

    terms = lax.dot_general(
        out_grad, kv_weight, (((1,), (1,)), ((), ())), preferred_element_type=jnp.float32
    ).astype(jnp.bfloat16)
    tokens, basis, terms = lax.optimization_barrier((tokens, basis, terms))
    input_grad = lax.psum_scatter(
        terms, "mp", scatter_dimension=0, axis_index_groups=GROUPS_X, tiled=True
    )
    input_grad = lax.psum_scatter(
        input_grad, "mp", scatter_dimension=0, axis_index_groups=GROUPS_Z, tiled=True
    )

    basis_t = basis.T.reshape(rank, n_mp, 2, half)
    mine = lax.dynamic_index_in_dim(basis_t, core, 2, keepdims=False).transpose(1, 0, 2)
    tok = tokens.reshape(rows, n_mp, 2, half)
    tok_mine = lax.dynamic_index_in_dim(tok, core, 2, keepdims=False).transpose(1, 0, 2)
    tok_other = lax.dynamic_index_in_dim(tok, 1 - core, 2, keepdims=False).transpose(1, 0, 2)
    got = lax.all_to_all(
        jnp.concatenate([mine, tok_mine, tok_other], axis=1), "mp", 0, 0, tiled=True
    )
    basis_mine = got[:, :rank].reshape(n_mp * rank, half)
    tok_mine = got[:, rank : rank + rows].reshape(n_tok, half)
    tok_other = got[:, rank + rows :].reshape(n_tok, half)
    basis_other = lax.ppermute(basis_mine, "dp", swap)
    nt = (((1,), (1,)), ((), ()))
    projected = lax.dot_general(
        basis_mine, tok_mine, nt, preferred_element_type=jnp.float32
    ) + lax.dot_general(basis_other, tok_other, nt, preferred_element_type=jnp.float32)
    projected = projected.astype(jnp.bfloat16).reshape(n_mp, rank, n_tok)

    got = lax.all_to_all(
        jnp.concatenate(
            [projected, jnp.broadcast_to(out_grad[None], (n_mp, n_tok, cols))], axis=1
        ),
        "mp",
        0,
        0,
        tiled=True,
    )
    projected = got[:, :rank].astype(jnp.float32).sum(0).astype(jnp.bfloat16)
    grad_all = got[:, rank:]
    partial_grad = jnp.einsum(
        "rt,jtc->jrc", projected, grad_all, preferred_element_type=jnp.float32
    )

    theirs = lax.ppermute(partial_grad.astype(jnp.bfloat16), "dp", swap)
    both = (partial_grad + theirs.astype(jnp.float32)).astype(jnp.bfloat16)
    got = lax.all_to_all(both, "dp", 0, 0, axis_index_groups=across, tiled=True)
    summed = got.astype(jnp.float32).sum(0)
    width_c = first_moment.shape[1]
    local_grad = lax.dynamic_slice_in_dim(summed, core * width_c, width_c, 1)

    new_first = 0.9 * first_moment + 0.1 * local_grad
    new_second = 0.999 * second_moment + 0.001 * local_grad * local_grad
    first_scale = 1.0 - 0.9**STEP
    second_scale = 1.0 - 0.999**STEP
    direction = (new_first / first_scale / (jnp.sqrt(new_second / second_scale) + epsilon)).astype(
        jnp.bfloat16
    )
    everyone = lax.all_to_all(
        jnp.broadcast_to(direction[None], (n_mp,) + direction.shape), "mp", 0, 0, tiled=True
    ).reshape(n_mp * rank, width_c)
    tn = (((0,), (0,)), ((), ()))
    up_mine = lax.dot_general(basis_mine, everyone, tn, preferred_element_type=jnp.float32)
    up_other = lax.dot_general(basis_other, everyone, tn, preferred_element_type=jnp.float32)
    first_half = jnp.where(core == 0, up_mine, up_other)
    second_half = jnp.where(core == 0, up_other, up_mine)
    update = jnp.concatenate([first_half, second_half], axis=0).astype(jnp.bfloat16)
    return (input_grad, update, new_first, new_second)


def solution(mesh):
    placed = (
        P(("dp", "mp"), None),
        P(None, "mp"),
        P("dp", "mp"),
        P(None, "mp"),
        P("mp", "dp"),
        P("mp", "dp"),
    )
    return jax.shard_map(
        body,
        mesh=mesh,
        in_specs=placed,
        out_specs=(P(("dp", "mp"), None), P("mp", "dp"), P("mp", "dp"), P("mp", "dp")),
        check_vma=False,
    )
```

time: 513 us -> 140 us (0.27)
  waiting for transfers between devices: 443 us -> 43.4 us
  starting transfers between devices: 0.16 us -> 36.5 us
  blocking collectives: 46.7 us -> 25.2 us
  local copies, waits for them, and re-layouts: 0.04 us -> 10.2 us
    psum x1 -> x0, waiting for transfers between devices: 225 us -> none  [body(): lax.psum(partial_grad.astype(jnp.bfloat16), 'dp').astype(jnp.float32)]
    reduce_scatter x2, waiting for transfers between devices: 191 us -> 0.01 us  [the longest x1 0.01 us: body(): lax.psum_scatter(terms, 'mp', scatter_dimension=0, axis_index_groups=GROU...]
    all_gather x1 -> x0, blocking collectives: 46.7 us -> none  [body(): grad_all = lax.all_gather(out_grad, 'mp', axis=1, tiled=True)]
    all_to_all x0 -> x3, waiting for transfers between devices: none -> 40.4 us  [the longest x1 16.4 us: body(): lax.all_to_all(jnp.concatenate([mine, tok_mine, tok_other], axis=1), 'mp'...]
    all_to_all x0 -> x3, starting transfers between devices: none -> 27.6 us  [the longest x1 13.4 us: body(): lax.all_to_all(jnp.concatenate([mine, tok_mine, tok_other], axis=1), 'mp'...]
    all_gather x1 -> x0, waiting for transfers between devices: 26.4 us -> none  [body(): lax.all_gather(tokens, 'mp', axis=0, tiled=True)]
    all_to_all x0 -> x1, blocking collectives: none -> 25.2 us  [body(): lax.all_to_all(jnp.concatenate([projected, jnp.broadcast_to(out_grad[None...]
    ppermute x0 -> x2, starting transfers between devices: none -> 8.8 us  [the longest x1 4.71 us: body(): theirs = lax.ppermute(partial_grad.astype(jnp.bfloat16), 'dp', swap)]
  transfers between devices with their start and end apart: 4 -> 7, of which waited for: 4 -> 5; matrix products, arithmetic and copies ran while one was open for 1% -> 8% of each run, Pallas kernels for 0% -> 0%
where the time goes in v1:
time: 140 us; the launch traced here: 139 us
  waiting for transfers between devices  43.4 us (31%)
  starting transfers between devices  36.5 us (26%)
  blocking collectives  25.2 us (18%)
  between operations  14.3 us (10%)
  local copies, waits for them, and re-layouts  10.2 us (7%)
  matrix products  4.96 us (4%)
  other arithmetic  4.56 us (3%)
    all_to_all x1, blocking collectives, body(): lax.all_to_all(jnp.concatenate([projected, jnp.broadcast_to(out_grad[None...  25.2 us
    all_to_all x1, waiting for transfers between devices, body(): lax.all_to_all(jnp.concatenate([mine, tok_mine, tok_other], axis=1), 'mp'...  16.4 us
    all_to_all x1, starting transfers between devices, body(): lax.all_to_all(jnp.concatenate([mine, tok_mine, tok_other], axis=1), 'mp'...  13.4 us
    all_to_all x1, waiting for transfers between devices, body(): lax.all_to_all(jnp.broadcast_to(direction[None], (n_mp,) + direction.shap...  13.1 us
    all_to_all x1, waiting for transfers between devices, body(): got = lax.all_to_all(both, 'dp', 0, 0, axis_index_groups=across, tiled=True)  10.9 us
    all_to_all x1, starting transfers between devices, body(): got = lax.all_to_all(both, 'dp', 0, 0, axis_index_groups=across, tiled=True)  10 us
    ppermute x1, starting transfers between devices, body(): theirs = lax.ppermute(partial_grad.astype(jnp.bfloat16), 'dp', swap)  4.71 us
    unnamed x10, local copies, waits for them, and re-layouts  4.22 us
  transfers between devices with their start and end apart: 7, of which 5 were waited for; matrix products, arithmetic and copies ran while one was open for 8% of the time, Pallas kernels for 0%

profile of v1, /device:TPU:1, one launch (start us, length us, event | category | flops | bytes accessed | tf_op | source)
XLA Modules:
  0.0 139.1 jit_solution(4445632925401206237)
XLA Ops:
  7.2 0.0 copy-start
  7.2 1.6 %copy-done = bf16[8192,128]{1,0:T(8,128)(2,1)S(1)} copy-done((bf16[8192,128]{1,0:T(8,128)(2,1)S(1)}, bf16[8192,128]{1,0:T(8,128)(2,1)}, u32[]{:S(2)}) %copy-start) | copy-done | bytes 2097176
  8.8 2.8 %convolution_convert_fusion = bf16[128,8192]{1,0:T(8,128)(2,1)} fusion(bf16[128,128]{1,0:T(8,128)(2,1)} %param.8, bf16[8192,128]{1,0:T(8,128)(2,1)S(1)} %copy-done), kind=kOutput, calls=%fused_computation | convolution fusion | flops 269484032 | bytes 4227072 | tf_op jit(solution)/shard_map/dot_general | solution.py:28
  11.6 1.8 %reshape.31 = bf16[64,16,2,256]{3,2,1,0:T(2,128)(2,1)S(1)} reshape(bf16[64,8192]{1,0:T(8,128)(2,1)} %bitcast.52) | data formatting | bytes 2097152 | tf_op jit(solution)/shard_map/reshape | solution.py:39
  13.4 0.0 copy-start.2
  13.4 1.2 constant_dynamic-slice_fusion
  14.7 0.6 copy.23
  15.2 0.0 copy-done.2
  15.3 0.9 pad_maximum_fusion.1
  16.2 13.4 %all-to-all-start = ((bf16[16,80,256]{2,1,0:T(8,128)(2,1)}), bf16[16,80,256]{2,1,0:T(8,128)(2,1)S(1)}, u32[]{:S(2)}, u32[]{:S(2)}) async-start(bf16[16,80,256]{2,1,0:T(8,128)(2,1)} %pad_maximum_fusion.1), calls=%async_computation.2 | async-start | bytes 1310720 | tf_op jit(solution)/shard_map/all_to_all | solution.py:44
  29.6 0.0 reduce-scatter.3.cloned.1.call-start
  29.7 0.7 reduce-scatter.3.cloned.1.call-update
  30.3 0.0 copy-start.1
  30.4 16.4 %all-to-all-done = bf16[16,80,256]{2,1,0:T(8,128)(2,1)S(1)} async-done(((bf16[16,80,256]{2,1,0:T(8,128)(2,1)}), bf16[16,80,256]{2,1,0:T(8,128)(2,1)S(1)}, u32[]{:S(2)}, u32[]{:S(2)}) %all-to-all-start) | async-done | bytes 655392 | tf_op jit(solution)/shard_map/all_to_all | solution.py:44
  46.8 4.1 %collective-permute-start = (bf16[1024,256]{1,0:T(8,128)(2,1)S(1)}, bf16[1024,256]{1,0:T(8,128)(2,1)S(1)}, u32[]{:S(2)}, u32[]{:S(2)}) collective-permute-start(bf16[1024,256]{1,0:T(8,128)(2,1)S(1)} %bitcast.50), channel_id=1, source_target_pairs={{0,16},{16,0},{32,48},{48,32},{64,80},{80,64},{96,112},{112,96},{1... | collective-permute-start | bytes 1572872 | tf_op jit(solution)/shard_map/ppermute | solution.py:50
  50.9 0.3 fusion.2
  51.2 1.2 collective-permute-done
  52.4 0.3 fusion
  52.7 0.0 copy-done.1
  52.7 0.1 broadcast_in_dim.4
  52.8 0.1 pad_maximum_fusion
  52.9 25.2 %all_to_all.20 = bf16[16,192,128]{2,1,0:T(8,128)(2,1)S(1)} all-to-all(bf16[16,192,128]{2,1,0:T(8,128)(2,1)S(1)} %pad_maximum_fusion), channel_id=1, replica_groups=mesh['dp'=32,'mp'=16] {'mp'}, dimensions={0} | all-to-all | bytes 1572864 | tf_op jit(solution)/shard_map/all_to_all | solution.py:57
  78.1 0.2 fusion.7
  78.3 4.7 %collective-permute-start.1 = (bf16[16,64,128]{2,1,0:T(8,128)(2,1)S(1)}, bf16[16,64,128]{2,1,0:T(8,128)(2,1)S(1)}, u32[]{:S(2)}, u32[]{:S(2)}) collective-permute-start(bf16[16,64,128]{2,1,0:T(8,128)(2,1)S(1)} %get-tuple-element.17), channel_id=1, source_target_pairs={{0,16},{16,0},{32,48},{48,32},{64,80},{80,64},{96,112},{112,96},{1... | collective-permute-start | bytes 786440 | tf_op jit(solution)/shard_map/ppermute | solution.py:72
  83.0 1.1 collective-permute-done.1
  84.2 0.8 add_convert_fusion
  85.0 10.0 %all-to-all-start.2 = ((bf16[16,64,128]{2,1,0:T(8,128)(2,1)}), bf16[16,64,128]{2,1,0:T(8,128)(2,1)S(1)}, u32[]{:S(2)}, u32[]{:S(2)}) async-start(bf16[16,64,128]{2,1,0:T(8,128)(2,1)} %add_convert_fusion), calls=%async_computation.4 | async-start | bytes 524288 | tf_op jit(solution)/shard_map/all_to_all | solution.py:74
  95.0 0.0 reduce-scatter.5.cloned.1.call-start
  95.0 10.9 %all-to-all-done.2 = bf16[16,64,128]{2,1,0:T(8,128)(2,1)S(1)} async-done(((bf16[16,64,128]{2,1,0:T(8,128)(2,1)}), bf16[16,64,128]{2,1,0:T(8,128)(2,1)S(1)}, u32[]{:S(2)}, u32[]{:S(2)}) %all-to-all-start.2) | async-done | bytes 262176 | tf_op jit(solution)/shard_map/all_to_all | solution.py:74
  106.0 0.7 convert_reduce_fusion
  106.6 0.0 reduce-scatter.3.cloned.1.call-done
  106.6 0.0 reduce-scatter.5.cloned.1.call-update
  106.7 1.5 %divide_convert_fusion = (bf16[64,64]{1,0:T(8,128)(2,1)S(1)}, f32[64,64]{1,0:T(8,128)}, f32[64,64]{1,0:T(8,128)}) fusion(f32[64,128]{1,0:T(8,128)} %convert_reduce_fusion, s32[]{:T(128)S(6)} %select_n.35, f32[64,64]{1,0:T(8,128)} %param.10, f32[64,64]{1,0:T(8,128)} %param.11), kind=kLoop, calls=%fused_computation.22 | loop fusion | flops 49152 | bytes 90116 | tf_op jit(solution)/shard_map/convert_element_type | solution.py:83
  108.2 0.1 copy.17
  108.2 0.1 broadcast_bitcast_fusion
  108.3 0.9 reshape.40
  109.2 4.2 %all-to-all-start.3 = ((bf16[16,2,2048]{2,1,0:T(2,128)(2,1)}), bf16[16,2,2048]{2,1,0:T(2,128)(2,1)}, u32[]{:S(2)}, u32[]{:S(2)}) async-start(bf16[16,2,2048]{2,1,0:T(2,128)(2,1)} %reshape.40), calls=%async_computation.5 | async-start | bytes 262144 | tf_op jit(solution)/shard_map/all_to_all | solution.py:86
  113.4 13.1 %all-to-all-done.3 = bf16[16,2,2048]{2,1,0:T(2,128)(2,1)} async-done(((bf16[16,2,2048]{2,1,0:T(2,128)(2,1)}), bf16[16,2,2048]{2,1,0:T(2,128)(2,1)}, u32[]{:S(2)}, u32[]{:S(2)}) %all-to-all-start.3) | async-done | bytes 131104 | tf_op jit(solution)/shard_map/all_to_all | solution.py:86
  126.5 1.1 reshape.41
  127.6 0.9 copy.18
  128.4 1.8 %reshape.37 = bf16[1024,64]{0,1:T(8,128)(2,1)} reshape(bf16[16,64,64]{1,0,2:T(8,128)(2,1)} %copy.18) | data formatting | bytes 262144 | tf_op jit(solution)/shard_map/reshape | solution.py:88
  130.2 0.2 convolution_bitcast_fusion.1
  130.5 1.1 select_convert_fusion.1
  131.6 0.6 pad_maximum_fusion.2
  132.2 0.0 reduce-scatter.5.cloned.1.call-done
  (3 shorter events, 0.1 us)
Async XLA Ops:
  7.2 1.6 %copy-start = (bf16[8192,128]{1,0:T(8,128)(2,1)S(1)}, bf16[8192,128]{1,0:T(8,128)(2,1)}, u32[]{:S(2)}) copy-start(bf16[8192,128]{1,0:T(8,128)(2,1)} %param.7) | copy-start | bytes 6291460
  13.4 1.8 %copy-start.2 = (bf16[8,8192]{1,0:T(8,128)(2,1)S(1)}, bf16[8,8192]{1,0:T(8,128)(2,1)}, u32[]{:S(2)}) copy-start(bf16[8,8192]{1,0:T(8,128)(2,1)} %param.6) | copy-start | bytes 393220
  16.2 30.5 %all-to-all-start = ((bf16[16,80,256]{2,1,0:T(8,128)(2,1)}), bf16[16,80,256]{2,1,0:T(8,128)(2,1)S(1)}, u32[]{:S(2)}, u32[]{:S(2)}) async-start(bf16[16,80,256]{2,1,0:T(8,128)(2,1)} %pad_maximum_fusion.1), calls=%async_computation.2 | async-start | bytes 1310720 | tf_op jit(solution)/shard_map/all_to_all | solution.py:44
  29.6 77.0 %reduce-scatter.3.cloned.1.call-start = ((), (), s32[]{:S(2)}) async-start(), calls=%async_computation.6 | async-start | bytes 2621440 | tf_op jit(solution)/shard_map/reduce_scatter | solution.py:32
  30.3 22.3 %copy-start.1 = (bf16[128,128]{1,0:T(8,128)(2,1)S(1)}, bf16[128,128]{1,0:T(8,128)(2,1)}, u32[]{:S(2)}) copy-start(bf16[128,128]{1,0:T(8,128)(2,1)} %param.8) | copy-start | bytes 98308
  46.8 5.6 %collective-permute-start = (bf16[1024,256]{1,0:T(8,128)(2,1)S(1)}, bf16[1024,256]{1,0:T(8,128)(2,1)S(1)}, u32[]{:S(2)}, u32[]{:S(2)}) collective-permute-start(bf16[1024,256]{1,0:T(8,128)(2,1)S(1)} %bitcast.50), channel_id=1, source_target_pairs={{0,16},{16,0},{32,48},{48,32},{64,80},{80,64},{96,112},{112,96},{1... | collective-permute-start | bytes 1572872 | tf_op jit(solution)/shard_map/ppermute | solution.py:50
  78.3 5.9 %collective-permute-start.1 = (bf16[16,64,128]{2,1,0:T(8,128)(2,1)S(1)}, bf16[16,64,128]{2,1,0:T(8,128)(2,1)S(1)}, u32[]{:S(2)}, u32[]{:S(2)}) collective-permute-start(bf16[16,64,128]{2,1,0:T(8,128)(2,1)S(1)} %get-tuple-element.17), channel_id=1, source_target_pairs={{0,16},{16,0},{32,48},{48,32},{64,80},{80,64},{96,112},{112,96},{1... | collective-permute-start | bytes 786440 | tf_op jit(solution)/shard_map/ppermute | solution.py:72
  85.0 21.0 %all-to-all-start.2 = ((bf16[16,64,128]{2,1,0:T(8,128)(2,1)}), bf16[16,64,128]{2,1,0:T(8,128)(2,1)S(1)}, u32[]{:S(2)}, u32[]{:S(2)}) async-start(bf16[16,64,128]{2,1,0:T(8,128)(2,1)} %add_convert_fusion), calls=%async_computation.4 | async-start | bytes 524288 | tf_op jit(solution)/shard_map/all_to_all | solution.py:74
  95.0 37.3 %reduce-scatter.5.cloned.1.call-start = ((), (), s32[]{:S(2)}) async-start(), calls=%async_computation.7 | async-start | bytes 655360 | tf_op jit(solution)/shard_map/reduce_scatter | solution.py:35
  109.2 17.2 %all-to-all-start.3 = ((bf16[16,2,2048]{2,1,0:T(2,128)(2,1)}), bf16[16,2,2048]{2,1,0:T(2,128)(2,1)}, u32[]{:S(2)}, u32[]{:S(2)}) async-start(bf16[16,2,2048]{2,1,0:T(2,128)(2,1)} %reshape.40), calls=%async_computation.5 | async-start | bytes 262144 | tf_op jit(solution)/shard_map/all_to_all | solution.py:86
Sparse Core Ops, SparseCore 0:
  33.3 44.5 reduce-scatter.2
  106.8 24.9 reduce-scatter.4

commit v2 on v0

v2 whole, which is shorter than its diff:
```python
import functools

import jax
import jax.numpy as jnp
from jax import lax
from jax.experimental import pallas as pl
from jax.experimental.pallas import tpu as pltpu
from jax.sharding import PartitionSpec as P

STEP = 10


epsilon = 1e-08

X, ZH, N_MP, N_DP, RANK = 4, 4, 16, 32, 64
ACROSS = [[2 * k + c for k in range(N_DP // 2)] for c in range(2)]
SWAP = [(d, d ^ 1) for d in range(N_DP)]
NT = (((1,), (1,)), ((), ()))
TN = (((0,), (0,)), ((), ()))
LIMIT = 48 * 2**20


def local(kernel, outs, *args, flops, moved, name):
    specs = [pl.BlockSpec(memory_space=pltpu.SMEM)] + [pl.BlockSpec(memory_space=pltpu.VMEM)] * (len(args) - 1)
    return pl.pallas_call(
        kernel,
        out_shape=outs,
        in_specs=specs,
        out_specs=jax.tree.map(lambda _: pl.BlockSpec(memory_space=pltpu.VMEM), outs),
        compiler_params=pltpu.CompilerParams(vmem_limit_bytes=LIMIT),
        cost_estimate=pl.CostEstimate(flops=flops, bytes_accessed=moved, transcendentals=0),
        name=name,
    )(*args)


def pack_rows(at_ref, basis_ref, tok_ref, out_ref):
    core = at_ref[0]
    rank, half = basis_ref.shape[0], out_ref.shape[2]
    for j in range(N_MP):
        mine = pl.ds(pl.multiple_of((2 * j + core) * half, half), half)
        other = pl.ds(pl.multiple_of((2 * j + 1 - core) * half, half), half)
        out_ref[j, :rank, :] = basis_ref[:, mine]
        out_ref[j, rank:, :] = jnp.concatenate([tok_ref[:, mine], tok_ref[:, other]], axis=0)


def adam(at_ref, got_ref, first_ref, second_ref, terms_ref, new_first_ref, new_second_ref, out_ref):
    core = at_ref[0]
    rank, width = first_ref.shape
    total = got_ref[0].astype(jnp.float32)
    for j in range(1, got_ref.shape[0]):
        total += got_ref[j].astype(jnp.float32)
    grad = jnp.where(core == 0, total[:, :width], total[:, width:])
    new_first = 0.9 * first_ref[...] + 0.1 * grad
    new_second = 0.999 * second_ref[...] + 0.001 * grad * grad
    new_first_ref[...] = new_first
    new_second_ref[...] = new_second
    first_scale = 1.0 - 0.9**STEP
    second_scale = 1.0 - 0.999**STEP
    direction = new_first / first_scale / (jnp.sqrt(new_second / second_scale) + epsilon)
    wide = jnp.concatenate([direction[: rank // 2], direction[rank // 2 :]], axis=1)
    rows = out_ref.shape[1]
    flat = jnp.concatenate(
        [wide[rows * b : rows * (b + 1)] for b in range(rank // 2 // rows)], axis=1
    ).astype(jnp.bfloat16)
    block = terms_ref.shape[2]
    for j in range(N_MP):
        out_ref[j, :, :block] = terms_ref[j]
        out_ref[j, :, block:] = flat


def finish(at_ref, mine_ref, other_ref, got_ref, input_grad_ref, update_ref):
    core = at_ref[0]
    cols, half = update_ref.shape[0], mine_ref.shape[2]
    rows, block = got_ref.shape[1], input_grad_ref.shape[1] // X
    lanes = 2 * cols
    for x in range(X):
        acc = got_ref[ZH * x, :, :block].astype(jnp.float32)
        for z in range(1, ZH):
            acc += got_ref[ZH * x + z, :, :block].astype(jnp.float32)
        input_grad_ref[:, block * x : block * (x + 1)] = acc.astype(input_grad_ref.dtype)
    parts = []
    for j in range(N_MP):
        flat = got_ref[j, :, block:].astype(jnp.float32)
        parts += [flat[:, lanes * b : lanes * (b + 1)] for b in range(RANK // 2 // rows)]
    direction = jnp.concatenate(parts, axis=0).astype(jnp.bfloat16)
    for where, ref in ((core, mine_ref), (1 - core, other_ref)):
        low = ref[:, : RANK // 2, :].reshape(N_MP * RANK // 2, half)
        high = ref[:, RANK // 2 : RANK, :].reshape(N_MP * RANK // 2, half)
        low = lax.dot_general(direction, low, TN, preferred_element_type=jnp.float32)
        high = lax.dot_general(direction, high, TN, preferred_element_type=jnp.float32)
        update_ref[:, pl.ds(pl.multiple_of(where * half, half), half)] = (
            low[:cols] + high[cols:]
        ).astype(update_ref.dtype)


def subspace(at_ref, got_ref, out_ref):
    total = got_ref[0, :RANK, :].astype(jnp.float32)
    for j in range(1, N_MP):
        total += got_ref[j, :RANK, :].astype(jnp.float32)
    projected = total.astype(jnp.bfloat16)
    for j in range(N_MP):
        out_ref[j] = jnp.dot(
            projected, got_ref[j, RANK:, :], preferred_element_type=jnp.float32
        ).astype(out_ref.dtype)


def grad_terms(at_ref, columns_ref, own_ref, *refs):
    core, x, z = at_ref[0], at_ref[1], at_ref[2]
    pieces, out_ref = refs[:-1], refs[-1]
    half = pieces[0].shape[0]
    grads = [columns_ref[((x + X - k) & (X - 1)) * ZH + z, RANK:, :] for k in range(X)]
    for where, refs in ((core, pieces[: X - 1]), (1 - core, pieces[X - 1 :])):
        rows = pl.ds(pl.multiple_of(where * half, half), half)
        acc = lax.dot_general(grads[0], own_ref[rows, :], NT, preferred_element_type=jnp.float32)
        for g, w in zip(grads[1:], refs):
            acc += lax.dot_general(g, w[...], NT, preferred_element_type=jnp.float32)
        out_ref[:, rows] = acc.astype(out_ref.dtype)


def body(tokens, kv_weight, out_grad, basis, first_moment, second_moment):
    bf16 = functools.partial(jax.ShapeDtypeStruct, dtype=jnp.bfloat16)
    f32 = functools.partial(jax.ShapeDtypeStruct, dtype=jnp.float32)
    rows, width = tokens.shape
    half = width // N_MP // 2
    n_tok, cols = out_grad.shape
    core = lax.axis_index("dp") & 1
    x, z = lax.axis_index("mp") // ZH, lax.axis_index("mp") % ZH
    at = jnp.stack([core, x, z])

    packed = local(
        pack_rows,
        bf16((N_MP, RANK + 2 * rows, half)),
        at,
        basis.T,
        tokens,
        flops=0,
        moved=2 * 2**20,
        name="pack_rows",
    )
    packed, kv_weight, out_grad = lax.optimization_barrier((packed, kv_weight, out_grad))
    mine = lax.all_to_all(packed, "mp", 0, 0, tiled=True)

    def along_x(a, k):
        return lax.ppermute(a, "mp", [(m, (m + ZH * k) % N_MP) for m in range(N_MP)])

    w_rows = width // X
    own = lax.dynamic_slice_in_dim(kv_weight, x * w_rows, w_rows, 0)

    def piece(k):
        start = (((x + k) & (X - 1)) * 2 + core) * (w_rows // 2)
        return along_x(lax.dynamic_slice_in_dim(kv_weight, start, w_rows // 2, 0), k)

    weight = [piece(k) for k in range(1, X)]
    mine, weight[0], weight[2] = lax.optimization_barrier((mine, weight[0], weight[2]))

    other = lax.ppermute(mine, "dp", SWAP)

    def block(a, lo, hi):
        return a[:, lo:hi].reshape(N_MP * (hi - lo), half)

    projected = lax.dot_general(
        block(mine, 0, RANK), block(mine, RANK, RANK + rows), NT, preferred_element_type=jnp.float32
    ) + lax.dot_general(
        block(other, 0, RANK),
        block(mine, RANK + rows, RANK + 2 * rows),
        NT,
        preferred_element_type=jnp.float32,
    )
    projected = projected.astype(jnp.bfloat16).reshape(N_MP, RANK, n_tok)

    columns = lax.all_to_all(
        jnp.concatenate(
            [projected, jnp.broadcast_to(out_grad[None], (N_MP, n_tok, cols))], axis=1
        ),
        "mp",
        0,
        0,
        tiled=True,
    )
    weight += [lax.ppermute(w, "dp", SWAP) for w in weight]
    columns, weight[1], weight[3], weight[5] = lax.optimization_barrier(
        (columns, weight[1], weight[3], weight[5])
    )
    partial_grad = local(
        subspace,
        bf16((N_MP, RANK, cols)),
        at,
        columns,
        flops=2**25,
        moved=2**20,
        name="subspace",
    )

    theirs = lax.ppermute(partial_grad, "dp", SWAP)
    both = (partial_grad.astype(jnp.float32) + theirs.astype(jnp.float32)).astype(jnp.bfloat16)
    both, columns = lax.optimization_barrier((both, columns))
    got = lax.all_to_all(both, "dp", 0, 0, axis_index_groups=ACROSS, tiled=True)

    terms = local(
        grad_terms,
        bf16((n_tok, width // X)),
        at,
        columns,
        own,
        *weight,
        flops=2 * n_tok * X * cols * width // X,
        moved=3 * 2**20,
        name="grad_terms",
    )
    packed_width = width // X + RANK // rows * first_moment.shape[1]
    new_first, new_second, packed = local(
        adam,
        (f32(first_moment.shape), f32(first_moment.shape), bf16((N_MP, rows, packed_width))),
        at,
        got,
        first_moment,
        second_moment,
        terms.reshape(N_MP, rows, width // X),
        flops=2**19,
        moved=2**20,
        name="adam",
    )
    input_grad, update = local(
        finish,
        (bf16((rows, width)), bf16((first_moment.shape[1], width // N_MP))),
        at,
        mine,
        other,
        lax.all_to_all(packed, "mp", 0, 0, tiled=True),
        flops=2 * 2**26,
        moved=2**21,
        name="finish",
    )
    return (input_grad, update.T, new_first, new_second)


def solution(mesh):
    placed = (
        P(("dp", "mp"), None),
        P(None, "mp"),
        P("dp", "mp"),
        P(None, "mp"),
        P("mp", "dp"),
        P("mp", "dp"),
    )
    return jax.shard_map(
        body,
        mesh=mesh,
        in_specs=placed,
        out_specs=(P(("dp", "mp"), None), P("mp", "dp"), P("mp", "dp"), P("mp", "dp")),
        check_vma=False,
    )
```

time: 513 us -> 127 us (0.25)
  waiting for transfers between devices: 443 us -> 24.7 us
  starting transfers between devices: 0.16 us -> 57.8 us
  blocking collectives: 46.7 us -> 24.6 us
  between operations: 13.8 us -> 0.89 us
  local copies, waits for them, and re-layouts: 0.04 us -> 8.15 us
  Pallas kernels: 0 us -> 6.79 us
  matrix products: 7.11 us -> 0.58 us
    psum x1 -> x0, waiting for transfers between devices: 225 us -> none  [body(): lax.psum(partial_grad.astype(jnp.bfloat16), 'dp').astype(jnp.float32)]
    reduce_scatter x2 -> x0, waiting for transfers between devices: 191 us -> none  [the longest x1 97.3 us: body(): lax.psum_scatter(lax.dot_general(out_grad, kv_weight, (((1,), (1,)), ((),...]
    all_gather x1 -> x0, blocking collectives: 46.7 us -> none  [body(): grad_all = lax.all_gather(out_grad, 'mp', axis=1, tiled=True)]
    all_to_all x0 -> x3, starting transfers between devices: none -> 32.4 us  [the longest x1 13.4 us: body(): mine = lax.all_to_all(packed, 'mp', 0, 0, tiled=True)]
    all_gather x1 -> x0, waiting for transfers between devices: 26.4 us -> none  [body(): lax.all_gather(tokens, 'mp', axis=0, tiled=True)]
    ppermute x0 -> x8, starting transfers between devices: none -> 25.4 us  [the longest x3 11.3 us: along_x(): lax.ppermute(a, 'mp', [(m, (m + ZH * k) % N_MP) for m in range(N_MP)])]
    all_to_all x0 -> x1, blocking collectives: none -> 24.6 us  [body(): lax.all_to_all(packed, 'mp', 0, 0, tiled=True)]
    ppermute x0 -> x8, waiting for transfers between devices: none -> 19.9 us  [the longest x3 17.2 us: along_x(): lax.ppermute(a, 'mp', [(m, (m + ZH * k) % N_MP) for m in range(N_MP)])]
  transfers between devices with their start and end apart: 4 -> 11, of which waited for: 4 -> 8; matrix products, arithmetic and copies ran while one was open for 1% -> 3% of each run, Pallas kernels for 0% -> 1%
where the time goes in v2:
time: 127 us; the launch traced here: 125 us
  starting transfers between devices  57.8 us (46%)
  waiting for transfers between devices  24.7 us (19%)
  blocking collectives  24.6 us (19%)
  local copies, waits for them, and re-layouts  8.15 us (6%)
  Pallas kernels  6.79 us (5%)
  other arithmetic  1.79 us (1%)
    all_to_all x1, blocking collectives, body(): lax.all_to_all(packed, 'mp', 0, 0, tiled=True)  24.6 us
    ppermute x3, waiting for transfers between devices, along_x(): lax.ppermute(a, 'mp', [(m, (m + ZH * k) % N_MP) for m in range(N_MP)])  17.2 us
    all_to_all x1, starting transfers between devices, body(): mine = lax.all_to_all(packed, 'mp', 0, 0, tiled=True)  13.4 us
    all_to_all x1, starting transfers between devices, body(): got = lax.all_to_all(both, 'dp', 0, 0, axis_index_groups=ACROSS, tiled=True)  11.9 us
    ppermute x3, starting transfers between devices, along_x(): lax.ppermute(a, 'mp', [(m, (m + ZH * k) % N_MP) for m in range(N_MP)])  11.3 us
    ppermute x3, starting transfers between devices, body(): weight += [lax.ppermute(w, 'dp', SWAP) for w in weight]  7.6 us
    all_to_all x1, starting transfers between devices, body(): lax.all_to_all(jnp.concatenate([projected, jnp.broadcast_to(out_grad[None...  7.11 us
    pallas_call x5, Pallas kernels, local(): pl.pallas_call(kernel, out_shape=outs, in_specs=specs, out_specs=jax.tree...  6.79 us
  transfers between devices with their start and end apart: 11, of which 8 were waited for; matrix products, arithmetic and copies ran while one was open for 3% of the time, Pallas kernels for 1%

profile of v2, /device:TPU:1, one launch (start us, length us, event | category | flops | bytes accessed | tf_op | source)
XLA Modules:
  0.0 125.4 jit_solution(15558100708069840604)
XLA Ops:
  0.7 0.1 pad_add_fusion.at_ref
  0.7 0.0 copy-start
  0.7 1.2 copy-done
  2.0 0.0 copy-start.7
  2.0 0.9 copy-done.7
  2.9 1.5 %pack_rows.1 = bf16[16,80,256]{2,1,0:T(8,128)(2,1)} custom-call(s32[3]{0:T(128)S(1)} %pad_add_fusion.at_ref, bf16[64,8192]{1,0:T(8,128)(2,1)S(1)} %bitcast.18, bf16[8,8192]{1,0:T(8,128)(2,1)S(1)} %copy-done.7), custom_call_target="tpu_custom_call" | custom-call | bytes 2097152 | tf_op jit(solution)/shard_map/pack_rows/pallas_call | solution.py:25
  4.3 13.4 %all-to-all-start = ((bf16[16,80,256]{2,1,0:T(8,128)(2,1)}), bf16[16,80,256]{2,1,0:T(8,128)(2,1)S(1)}, u32[]{:S(2)}, u32[]{:S(2)}) async-start(bf16[16,80,256]{2,1,0:T(8,128)(2,1)} %pack_rows.1), calls=%async_computation | async-start | bytes 1310720 | tf_op jit(solution)/shard_map/all_to_all | solution.py:141
  17.8 1.9 %constant_dynamic-slice_fusion.1 = (bf16[1024,128]{1,0:T(8,128)(2,1)}, bf16[1024,128]{1,0:T(8,128)(2,1)S(1)}, bf16[1024,128]{1,0:T(8,128)(2,1)S(1)}) fusion(bf16[8192,128]{1,0:T(8,128)(2,1)} %param.7, s32[]{:T(128)S(6)} %select_n.27, s32[]{:T(128)S(6)} %select_n.26, s32[]{:T(128)S(6)} %select_n.25), kind=kLoop, calls=%fused_computation.10 | loop fusion | bytes 1572876 | tf_op jit(solution)/shard_map/dynamic_slice | solution.py:151
  19.7 3.2 %collective-permute-start = (bf16[1024,128]{1,0:T(8,128)(2,1)S(1)}, bf16[1024,128]{1,0:T(8,128)(2,1)S(1)}, u32[]{:S(2)}, u32[]{:S(2)}) collective-permute-start(bf16[1024,128]{1,0:T(8,128)(2,1)S(1)} %get-tuple-element.40), channel_id=1, source_target_pairs={{0,4},{1,5},{2,6},{3,7},{4,8},{5,9},{6,10},{7,11},{8,12},{9,13},{1... | collective-permute-start | bytes 786440 | tf_op jit(solution)/shard_map/ppermute | solution.py:144
  22.9 0.0 copy-start.10
  22.9 3.2 %collective-permute-start.1 = (bf16[1024,128]{1,0:T(8,128)(2,1)S(1)}, bf16[1024,128]{1,0:T(8,128)(2,1)S(1)}, u32[]{:S(2)}, u32[]{:S(2)}) collective-permute-start(bf16[1024,128]{1,0:T(8,128)(2,1)S(1)} %get-tuple-element.39), channel_id=1, source_target_pairs={{0,12},{1,13},{2,14},{3,15},{4,0},{5,1},{6,2},{7,3},{8,4},{9,5},{1... | collective-permute-start | bytes 786440 | tf_op jit(solution)/shard_map/ppermute | solution.py:144
  26.2 7.2 %collective-permute-done.refs_0_ = bf16[1024,128]{1,0:T(8,128)(2,1)S(1)} collective-permute-done((bf16[1024,128]{1,0:T(8,128)(2,1)S(1)}, bf16[1024,128]{1,0:T(8,128)(2,1)S(1)}, u32[]{:S(2)}, u32[]{:S(2)}) %collective-permute-start) | collective-permute-done | bytes 262176 | tf_op jit(solution)/shard_map/ppermute | solution.py:144
  33.3 2.8 %collective-permute-done.1.refs_2_ = bf16[1024,128]{1,0:T(8,128)(2,1)S(1)} collective-permute-done((bf16[1024,128]{1,0:T(8,128)(2,1)S(1)}, bf16[1024,128]{1,0:T(8,128)(2,1)S(1)}, u32[]{:S(2)}, u32[]{:S(2)}) %collective-permute-start.1) | collective-permute-done | bytes 262176 | tf_op jit(solution)/shard_map/ppermute | solution.py:144
  36.1 0.0 all-to-all-done.mine_ref
  36.1 2.8 %collective-permute-start.2 = (bf16[16,80,256]{2,1,0:T(8,128)(2,1)S(1)}, bf16[16,80,256]{2,1,0:T(8,128)(2,1)S(1)}, u32[]{:S(2)}, u32[]{:S(2)}) collective-permute-start(bf16[16,80,256]{2,1,0:T(8,128)(2,1)S(1)} %all-to-all-done.mine_ref), channel_id=1, source_target_pairs={{0,16},{16,0},{32,48},{48,32},{64,80},{80,64},{96,112},{112,96},{1... | collective-permute-start | bytes 1966088 | tf_op jit(solution)/shard_map/ppermute | solution.py:156
  39.0 0.3 fusion.2
  39.3 1.4 %collective-permute-done.2.other_ref = bf16[16,80,256]{2,1,0:T(8,128)(2,1)S(1)} collective-permute-done((bf16[16,80,256]{2,1,0:T(8,128)(2,1)S(1)}, bf16[16,80,256]{2,1,0:T(8,128)(2,1)S(1)}, u32[]{:S(2)}, u32[]{:S(2)}) %collective-permute-start.2) | collective-permute-done | bytes 655392 | tf_op jit(solution)/shard_map/ppermute | solution.py:156
  40.7 0.3 fusion
  41.0 0.0 copy-done.10
  41.0 0.1 broadcast_in_dim.2
  41.1 0.9 pad_maximum_fusion
  42.1 7.1 %all-to-all-start.1 = ((bf16[16,192,128]{2,1,0:T(8,128)(2,1)}), bf16[16,192,128]{2,1,0:T(8,128)(2,1)S(1)}, u32[]{:S(2)}, u32[]{:S(2)}) async-start(bf16[16,192,128]{2,1,0:T(8,128)(2,1)} %pad_maximum_fusion), calls=%async_computation.1 | async-start | bytes 1572864 | tf_op jit(solution)/shard_map/all_to_all | solution.py:171
  49.2 4.8 %collective-permute-start.3 = (bf16[1024,128]{1,0:T(8,128)(2,1)}, bf16[1024,128]{1,0:T(8,128)(2,1)S(1)}, u32[]{:S(2)}, u32[]{:S(2)}) collective-permute-start(bf16[1024,128]{1,0:T(8,128)(2,1)} %get-tuple-element.38), channel_id=1, source_target_pairs={{0,8},{1,9},{2,10},{3,11},{4,12},{5,13},{6,14},{7,15},{8,0},{9,1},... | collective-permute-start | bytes 786440 | tf_op jit(solution)/shard_map/ppermute | solution.py:144
  54.0 3.1 %collective-permute-start.4 = (bf16[1024,128]{1,0:T(8,128)(2,1)S(1)}, bf16[1024,128]{1,0:T(8,128)(2,1)S(1)}, u32[]{:S(2)}, u32[]{:S(2)}) collective-permute-start(bf16[1024,128]{1,0:T(8,128)(2,1)S(1)} %collective-permute-done.refs_0_), channel_id=1, source_target_pairs={{0,16},{16,0},{32,48},{48,32},{64,80},{80,64},{96,112},{112,96},{1... | collective-permute-start | bytes 786440 | tf_op jit(solution)/shard_map/ppermute | solution.py:180
  57.1 1.9 %collective-permute-start.5 = (bf16[1024,128]{1,0:T(8,128)(2,1)S(1)}, bf16[1024,128]{1,0:T(8,128)(2,1)S(1)}, u32[]{:S(2)}, u32[]{:S(2)}) collective-permute-start(bf16[1024,128]{1,0:T(8,128)(2,1)S(1)} %collective-permute-done.1.refs_2_), channel_id=1, source_target_pairs={{0,16},{16,0},{32,48},{48,32},{64,80},{80,64},{96,112},{112,96},{1... | collective-permute-start | bytes 786440 | tf_op jit(solution)/shard_map/ppermute | solution.py:180
  59.0 7.3 %collective-permute-done.3.refs_1_ = bf16[1024,128]{1,0:T(8,128)(2,1)S(1)} collective-permute-done((bf16[1024,128]{1,0:T(8,128)(2,1)}, bf16[1024,128]{1,0:T(8,128)(2,1)S(1)}, u32[]{:S(2)}, u32[]{:S(2)}) %collective-permute-start.3) | collective-permute-done | bytes 262176 | tf_op jit(solution)/shard_map/ppermute | solution.py:144
  66.3 0.0 copy-start.1
  66.3 0.0 collective-permute-done.4.refs_3_
  66.3 0.0 copy-start.3
  66.3 0.0 collective-permute-done.5.refs_5_
  66.3 0.0 copy-start.5
  66.3 2.2 %all-to-all-done.1.got_ref.columns_ref = bf16[16,192,128]{2,1,0:T(8,128)(2,1)S(1)} async-done(((bf16[16,192,128]{2,1,0:T(8,128)(2,1)}), bf16[16,192,128]{2,1,0:T(8,128)(2,1)S(1)}, u32[]{:S(2)}, u32[]{:S(2)}) %all-to-all-start.1) | async-done | bytes 786464 | tf_op jit(solution)/shard_map/all_to_all | solution.py:171
  68.6 0.8 subspace.1
  69.4 3.8 %collective-permute-start.6 = (bf16[16,64,128]{2,1,0:T(8,128)(2,1)S(1)}, bf16[16,64,128]{2,1,0:T(8,128)(2,1)S(1)}, u32[]{:S(2)}, u32[]{:S(2)}) collective-permute-start(bf16[16,64,128]{2,1,0:T(8,128)(2,1)S(1)} %subspace.1), channel_id=1, source_target_pairs={{0,16},{16,0},{32,48},{48,32},{64,80},{80,64},{96,112},{112,96},{1... | collective-permute-start | bytes 786440 | tf_op jit(solution)/shard_map/ppermute | solution.py:194
  73.1 1.1 collective-permute-done.6
  74.3 0.8 add_convert_fusion
  75.1 0.0 copy-done.5
  75.1 11.9 %all-to-all-start.2 = ((bf16[16,64,128]{2,1,0:T(8,128)(2,1)}), bf16[16,64,128]{2,1,0:T(8,128)(2,1)S(1)}, u32[]{:S(2)}, u32[]{:S(2)}) async-start(bf16[16,64,128]{2,1,0:T(8,128)(2,1)} %add_convert_fusion), calls=%async_computation.2 | async-start | bytes 524288 | tf_op jit(solution)/shard_map/all_to_all | solution.py:197
  86.9 2.6 %collective-permute-start.7 = (bf16[1024,128]{1,0:T(8,128)(2,1)S(1)}, bf16[1024,128]{1,0:T(8,128)(2,1)}, u32[]{:S(2)}, u32[]{:S(2)}) collective-permute-start(bf16[1024,128]{1,0:T(8,128)(2,1)S(1)} %collective-permute-done.3.refs_1_), channel_id=1, source_target_pairs={{0,16},{16,0},{32,48},{48,32},{64,80},{80,64},{96,112},{112,96},{1... | collective-permute-start | bytes 786440 | tf_op jit(solution)/shard_map/ppermute | solution.py:180
  89.5 0.0 copy-start.8
  89.5 0.0 copy-start.9
  89.5 1.1 constant_dynamic-slice_fusion.own_ref
  90.6 0.0 copy-done.1
  90.6 0.0 copy-done.3
  90.6 0.1 collective-permute-done.7.refs_4_
  90.8 0.0 copy-start.2
  90.8 0.9 copy-done.2
  91.7 0.0 copy-start.4
  91.7 0.9 copy-done.4
  92.7 0.0 copy-start.6
  92.7 0.9 copy-done.6
  93.6 1.7 %grad_terms.1 = bf16[128,2048]{1,0:T(8,128)(2,1)S(1)} custom-call(s32[3]{0:T(128)S(1)} %pad_add_fusion.at_ref, bf16[16,192,128]{2,1,0:T(8,128)(2,1)S(1)} %all-to-all-done.1.got_ref.columns_ref, bf16[2048,128]{1,0:T(8,128)(2,1)S(1)} %constant_dynamic-slice_fusion.own_ref, bf16[1024,128]{1,0:T(8,128)(2,1)S(1)} %collective-permute-done.refs_0_, ...), custom_call_target="tpu_custom_call" | custom-call | flops 268435456 | bytes 3145728 | tf_op jit(solution)/shard_map/grad_terms/pallas_call | solution.py:25
  95.3 2.6 %all-to-all-done.2.got_ref = bf16[16,64,128]{2,1,0:T(8,128)(2,1)S(1)} async-done(((bf16[16,64,128]{2,1,0:T(8,128)(2,1)}), bf16[16,64,128]{2,1,0:T(8,128)(2,1)S(1)}, u32[]{:S(2)}, u32[]{:S(2)}) %all-to-all-start.2) | async-done | bytes 262176 | tf_op jit(solution)/shard_map/all_to_all | solution.py:197
  97.9 0.0 copy-done.8
  97.9 0.0 copy-done.9
  97.9 1.3 %adam.1 = (f32[64,64]{1,0:T(8,128)}, f32[64,64]{1,0:T(8,128)}, bf16[16,8,2560]{2,1,0:T(8,128)(2,1)S(1)}) custom-call(s32[3]{0:T(128)S(1)} %pad_add_fusion.at_ref, bf16[16,64,128]{2,1,0:T(8,128)(2,1)S(1)} %all-to-all-done.2.got_ref, f32[64,64]{1,0:T(8,128)S(1)} %copy-done.8, f32[64,64]{1,0:T(8,128)S(1)} %copy-done.9, bf16[16,8,2048]{2,1,0:T(8,128)(2,1)S(1)} %bitcast.17), custom_call_target="tpu_custom_call" | custom-call | flops 524288 | bytes 1048576 | tf_op jit(solution)/shard_map/adam/pallas_call | solution.py:25
  99.2 24.6 %all_to_all.20.got_ref = bf16[16,8,2560]{2,1,0:T(8,128)(2,1)S(1)} all-to-all(bf16[16,8,2560]{2,1,0:T(8,128)(2,1)S(1)} %get-tuple-element.33), channel_id=1, replica_groups=mesh['dp'=32,'mp'=16] {'mp'}, dimensions={0} | all-to-all | bytes 1310720 | tf_op jit(solution)/shard_map/all_to_all | solution.py:229
  123.8 1.5 %finish.1 = (bf16[8,8192]{1,0:T(8,128)(2,1)}, bf16[64,512]{1,0:T(8,128)(2,1)}) custom-call(s32[3]{0:T(128)S(1)} %pad_add_fusion.at_ref, bf16[16,80,256]{2,1,0:T(8,128)(2,1)S(1)} %all-to-all-done.mine_ref, bf16[16,80,256]{2,1,0:T(8,128)(2,1)S(1)} %collective-permute-done.2.other_ref, bf16[16,8,2560]{2,1,0:T(8,128)(2,1)S(1)} %all_to_all.20.got_ref), custom_call_target="tpu_custom_call" | custom-call | flops 134217728 | bytes 2097152 | tf_op jit(solution)/shard_map/finish/pallas_call | solution.py:25
  (2 shorter events, 0.1 us)
Async XLA Ops:
  0.7 1.2 copy-start
  2.0 0.9 copy-start.7
  4.3 31.8 %all-to-all-start = ((bf16[16,80,256]{2,1,0:T(8,128)(2,1)}), bf16[16,80,256]{2,1,0:T(8,128)(2,1)S(1)}, u32[]{:S(2)}, u32[]{:S(2)}) async-start(bf16[16,80,256]{2,1,0:T(8,128)(2,1)} %pack_rows.1), calls=%async_computation | async-start | bytes 1310720 | tf_op jit(solution)/shard_map/all_to_all | solution.py:141
  19.7 13.7 %collective-permute-start = (bf16[1024,128]{1,0:T(8,128)(2,1)S(1)}, bf16[1024,128]{1,0:T(8,128)(2,1)S(1)}, u32[]{:S(2)}, u32[]{:S(2)}) collective-permute-start(bf16[1024,128]{1,0:T(8,128)(2,1)S(1)} %get-tuple-element.40), channel_id=1, source_target_pairs={{0,4},{1,5},{2,6},{3,7},{4,8},{5,9},{6,10},{7,11},{8,12},{9,13},{1... | collective-permute-start | bytes 786440 | tf_op jit(solution)/shard_map/ppermute | solution.py:144
  22.9 18.1 %copy-start.10 = (bf16[128,128]{1,0:T(8,128)(2,1)S(1)}, bf16[128,128]{1,0:T(8,128)(2,1)}, u32[]{:S(2)}) copy-start(bf16[128,128]{1,0:T(8,128)(2,1)} %param.8) | copy-start | bytes 98308
  22.9 13.2 %collective-permute-start.1 = (bf16[1024,128]{1,0:T(8,128)(2,1)S(1)}, bf16[1024,128]{1,0:T(8,128)(2,1)S(1)}, u32[]{:S(2)}, u32[]{:S(2)}) collective-permute-start(bf16[1024,128]{1,0:T(8,128)(2,1)S(1)} %get-tuple-element.39), channel_id=1, source_target_pairs={{0,12},{1,13},{2,14},{3,15},{4,0},{5,1},{6,2},{7,3},{8,4},{9,5},{1... | collective-permute-start | bytes 786440 | tf_op jit(solution)/shard_map/ppermute | solution.py:144
  36.1 4.5 %collective-permute-start.2 = (bf16[16,80,256]{2,1,0:T(8,128)(2,1)S(1)}, bf16[16,80,256]{2,1,0:T(8,128)(2,1)S(1)}, u32[]{:S(2)}, u32[]{:S(2)}) collective-permute-start(bf16[16,80,256]{2,1,0:T(8,128)(2,1)S(1)} %all-to-all-done.mine_ref), channel_id=1, source_target_pairs={{0,16},{16,0},{32,48},{48,32},{64,80},{80,64},{96,112},{112,96},{1... | collective-permute-start | bytes 1966088 | tf_op jit(solution)/shard_map/ppermute | solution.py:156
  42.1 26.5 %all-to-all-start.1 = ((bf16[16,192,128]{2,1,0:T(8,128)(2,1)}), bf16[16,192,128]{2,1,0:T(8,128)(2,1)S(1)}, u32[]{:S(2)}, u32[]{:S(2)}) async-start(bf16[16,192,128]{2,1,0:T(8,128)(2,1)} %pad_maximum_fusion), calls=%async_computation.1 | async-start | bytes 1572864 | tf_op jit(solution)/shard_map/all_to_all | solution.py:171
  49.2 17.1 %collective-permute-start.3 = (bf16[1024,128]{1,0:T(8,128)(2,1)}, bf16[1024,128]{1,0:T(8,128)(2,1)S(1)}, u32[]{:S(2)}, u32[]{:S(2)}) collective-permute-start(bf16[1024,128]{1,0:T(8,128)(2,1)} %get-tuple-element.38), channel_id=1, source_target_pairs={{0,8},{1,9},{2,10},{3,11},{4,12},{5,13},{6,14},{7,15},{8,0},{9,1},... | collective-permute-start | bytes 786440 | tf_op jit(solution)/shard_map/ppermute | solution.py:144
  54.0 12.3 %collective-permute-start.4 = (bf16[1024,128]{1,0:T(8,128)(2,1)S(1)}, bf16[1024,128]{1,0:T(8,128)(2,1)S(1)}, u32[]{:S(2)}, u32[]{:S(2)}) collective-permute-start(bf16[1024,128]{1,0:T(8,128)(2,1)S(1)} %collective-permute-done.refs_0_), channel_id=1, source_target_pairs={{0,16},{16,0},{32,48},{48,32},{64,80},{80,64},{96,112},{112,96},{1... | collective-permute-start | bytes 786440 | tf_op jit(solution)/shard_map/ppermute | solution.py:180
  57.1 9.2 %collective-permute-start.5 = (bf16[1024,128]{1,0:T(8,128)(2,1)S(1)}, bf16[1024,128]{1,0:T(8,128)(2,1)S(1)}, u32[]{:S(2)}, u32[]{:S(2)}) collective-permute-start(bf16[1024,128]{1,0:T(8,128)(2,1)S(1)} %collective-permute-done.1.refs_2_), channel_id=1, source_target_pairs={{0,16},{16,0},{32,48},{48,32},{64,80},{80,64},{96,112},{112,96},{1... | collective-permute-start | bytes 786440 | tf_op jit(solution)/shard_map/ppermute | solution.py:180
  66.3 24.3 %copy-start.1 = (bf16[1024,128]{1,0:T(8,128)(2,1)}, bf16[1024,128]{1,0:T(8,128)(2,1)S(1)}, u32[]{:S(2)}) copy-start(bf16[1024,128]{1,0:T(8,128)(2,1)S(1)} %collective-permute-done.3.refs_1_) | copy-start | bytes 786436
  66.3 24.3 %copy-start.3 = (bf16[1024,128]{1,0:T(8,128)(2,1)}, bf16[1024,128]{1,0:T(8,128)(2,1)S(1)}, u32[]{:S(2)}) copy-start(bf16[1024,128]{1,0:T(8,128)(2,1)S(1)} %collective-permute-done.4.refs_3_) | copy-start | bytes 786436
  66.3 8.7 %copy-start.5 = (bf16[1024,128]{1,0:T(8,128)(2,1)}, bf16[1024,128]{1,0:T(8,128)(2,1)S(1)}, u32[]{:S(2)}) copy-start(bf16[1024,128]{1,0:T(8,128)(2,1)S(1)} %collective-permute-done.5.refs_5_) | copy-start | bytes 786436
  69.4 4.9 %collective-permute-start.6 = (bf16[16,64,128]{2,1,0:T(8,128)(2,1)S(1)}, bf16[16,64,128]{2,1,0:T(8,128)(2,1)S(1)}, u32[]{:S(2)}, u32[]{:S(2)}) collective-permute-start(bf16[16,64,128]{2,1,0:T(8,128)(2,1)S(1)} %subspace.1), channel_id=1, source_target_pairs={{0,16},{16,0},{32,48},{48,32},{64,80},{80,64},{96,112},{112,96},{1... | collective-permute-start | bytes 786440 | tf_op jit(solution)/shard_map/ppermute | solution.py:194
  75.1 22.9 %all-to-all-start.2 = ((bf16[16,64,128]{2,1,0:T(8,128)(2,1)}), bf16[16,64,128]{2,1,0:T(8,128)(2,1)S(1)}, u32[]{:S(2)}, u32[]{:S(2)}) async-start(bf16[16,64,128]{2,1,0:T(8,128)(2,1)} %add_convert_fusion), calls=%async_computation.2 | async-start | bytes 524288 | tf_op jit(solution)/shard_map/all_to_all | solution.py:197
  86.9 3.8 %collective-permute-start.7 = (bf16[1024,128]{1,0:T(8,128)(2,1)S(1)}, bf16[1024,128]{1,0:T(8,128)(2,1)}, u32[]{:S(2)}, u32[]{:S(2)}) collective-permute-start(bf16[1024,128]{1,0:T(8,128)(2,1)S(1)} %collective-permute-done.3.refs_1_), channel_id=1, source_target_pairs={{0,16},{16,0},{32,48},{48,32},{64,80},{80,64},{96,112},{112,96},{1... | collective-permute-start | bytes 786440 | tf_op jit(solution)/shard_map/ppermute | solution.py:180
  89.5 8.4 %copy-start.8 = (f32[64,64]{1,0:T(8,128)S(1)}, f32[64,64]{1,0:T(8,128)}, u32[]{:S(2)}) copy-start(f32[64,64]{1,0:T(8,128)} %first_ref.1) | copy-start | bytes 49156
  89.5 8.4 %copy-start.9 = (f32[64,64]{1,0:T(8,128)S(1)}, f32[64,64]{1,0:T(8,128)}, u32[]{:S(2)}) copy-start(f32[64,64]{1,0:T(8,128)} %second_ref.1) | copy-start | bytes 49156
  90.8 0.9 copy-start.2
  91.7 0.9 copy-start.4
  92.7 0.9 copy-start.6

commit v3 on v2

v3 whole, which is shorter than its diff:
```python
import functools

import jax
import jax.numpy as jnp
from jax import lax
from jax.experimental import pallas as pl
from jax.experimental.pallas import tpu as pltpu
from jax.sharding import PartitionSpec as P

STEP = 10


epsilon = 1e-08

X, ZH, N_MP, N_DP, RANK = 4, 4, 16, 32, 64
GROUPS_X = [[z + ZH * x for x in range(X)] for z in range(ZH)]
GROUPS_Z = [[z + ZH * x for z in range(ZH)] for x in range(X)]
ACROSS = [[2 * k + c for k in range(N_DP // 2)] for c in range(2)]
SWAP = [(d, d ^ 1) for d in range(N_DP)]
NT = (((1,), (1,)), ((), ()))
TN = (((0,), (0,)), ((), ()))
LIMIT = 48 * 2**20


VMEM = pl.BlockSpec(memory_space=pltpu.VMEM)
HBM = pl.BlockSpec(memory_space=pltpu.HBM)


def local(kernel, outs, *args, ins, scratch=(), limit=LIMIT, flops=0, moved=0, name):
    return pl.pallas_call(
        kernel,
        out_shape=outs,
        in_specs=[pl.BlockSpec(memory_space=pltpu.SMEM), *ins],
        out_specs=jax.tree.map(lambda _: VMEM, outs),
        scratch_shapes=scratch,
        compiler_params=pltpu.CompilerParams(vmem_limit_bytes=limit),
        cost_estimate=pl.CostEstimate(flops=flops, bytes_accessed=moved, transcendentals=0),
        name=name,
    )(*args)


def pack_rows(at_ref, basis_ref, tok_ref, out_ref, tok, sems):
    core = at_ref[0]
    half = out_ref.shape[2]
    first = pltpu.make_async_copy(tok_ref, tok, sems.at[0])
    first.start()
    copies = []
    for j in range(N_MP):
        mine = pl.ds(pl.multiple_of((2 * j + core) * half, half), half)
        copies.append(
            pltpu.make_async_copy(basis_ref.at[:, mine], out_ref.at[j, pl.ds(0, RANK), :], sems.at[1])
        )
    for copy in copies:
        copy.start()
    first.wait()
    for j in range(N_MP):
        mine = pl.ds(pl.multiple_of((2 * j + core) * half, half), half)
        other = pl.ds(pl.multiple_of((2 * j + 1 - core) * half, half), half)
        out_ref[j, RANK:, :] = jnp.concatenate([tok[:, mine], tok[:, other]], axis=0)
    for copy in copies:
        copy.wait()


def adam(at_ref, got_ref, first_ref, second_ref, new_first_ref, new_second_ref, out_ref):
    core = at_ref[0]
    rank, width = first_ref.shape
    total = got_ref[0].astype(jnp.float32)
    for j in range(1, got_ref.shape[0]):
        total += got_ref[j].astype(jnp.float32)
    grad = jnp.where(core == 0, total[:, :width], total[:, width:])
    new_first = 0.9 * first_ref[...] + 0.1 * grad
    new_second = 0.999 * second_ref[...] + 0.001 * grad * grad
    new_first_ref[...] = new_first
    new_second_ref[...] = new_second
    first_scale = 1.0 - 0.9**STEP
    second_scale = 1.0 - 0.999**STEP
    direction = new_first / first_scale / (jnp.sqrt(new_second / second_scale) + epsilon)
    wide = jnp.concatenate([direction[: rank // 2], direction[rank // 2 :]], axis=1)
    rows = out_ref.shape[1]
    flat = jnp.concatenate(
        [wide[rows * b : rows * (b + 1)] for b in range(rank // 2 // rows)], axis=1
    ).astype(jnp.bfloat16)
    for j in range(N_MP):
        out_ref[j] = flat


def back_project(at_ref, mine_ref, other_ref, got_ref, update_ref):
    core = at_ref[0]
    cols, half = update_ref.shape[0], mine_ref.shape[2]
    rows = got_ref.shape[1]
    lanes = 2 * cols
    parts = []
    for j in range(N_MP):
        flat = got_ref[j].astype(jnp.float32)
        parts += [flat[:, lanes * b : lanes * (b + 1)] for b in range(RANK // 2 // rows)]
    direction = jnp.concatenate(parts, axis=0).astype(jnp.bfloat16)
    for where, ref in ((core, mine_ref), (1 - core, other_ref)):
        low = ref[:, : RANK // 2, :].reshape(N_MP * RANK // 2, half)
        high = ref[:, RANK // 2 : RANK, :].reshape(N_MP * RANK // 2, half)
        low = lax.dot_general(direction, low, TN, preferred_element_type=jnp.float32)
        high = lax.dot_general(direction, high, TN, preferred_element_type=jnp.float32)
        update_ref[:, pl.ds(pl.multiple_of(where * half, half), half)] = (
            low[:cols] + high[cols:]
        ).astype(update_ref.dtype)


def subspace(at_ref, got_ref, out_ref):
    total = got_ref[0, :RANK, :].astype(jnp.float32)
    for j in range(1, N_MP):
        total += got_ref[j, :RANK, :].astype(jnp.float32)
    projected = total.astype(jnp.bfloat16)
    for j in range(N_MP):
        out_ref[j] = jnp.dot(
            projected, got_ref[j, RANK:, :], preferred_element_type=jnp.float32
        ).astype(out_ref.dtype)


def body(tokens, kv_weight, out_grad, basis, first_moment, second_moment):
    bf16 = functools.partial(jax.ShapeDtypeStruct, dtype=jnp.bfloat16)
    f32 = functools.partial(jax.ShapeDtypeStruct, dtype=jnp.float32)
    rows, width = tokens.shape
    half = width // N_MP // 2
    n_tok, cols = out_grad.shape
    at = (lax.axis_index("dp") & 1)[None]

    packed = local(
        pack_rows,
        bf16((N_MP, RANK + 2 * rows, half)),
        at,
        basis.T,
        tokens,
        ins=[HBM] * 2,
        scratch=[pltpu.VMEM((rows, width), jnp.bfloat16), pltpu.SemaphoreType.DMA((2,))],
        limit=60 * 2**20,
        flops=0,
        moved=2 * 2**20,
        name="pack_rows",
    )
    packed, kv_weight, out_grad = lax.optimization_barrier((packed, kv_weight, out_grad))
    mine = lax.all_to_all(packed, "mp", 0, 0, tiled=True)

    terms = lax.dot_general(
        out_grad, kv_weight, (((1,), (1,)), ((), ())), preferred_element_type=jnp.float32
    ).astype(jnp.bfloat16)
    input_grad = lax.psum_scatter(
        terms, "mp", scatter_dimension=0, axis_index_groups=GROUPS_X, tiled=True
    )

    other = lax.ppermute(mine, "dp", SWAP)

    def block(a, lo, hi):
        return a[:, lo:hi].reshape(N_MP * (hi - lo), half)

    projected = lax.dot_general(
        block(mine, 0, RANK), block(mine, RANK, RANK + rows), NT, preferred_element_type=jnp.float32
    ) + lax.dot_general(
        block(other, 0, RANK),
        block(mine, RANK + rows, RANK + 2 * rows),
        NT,
        preferred_element_type=jnp.float32,
    )
    projected = projected.astype(jnp.bfloat16).reshape(N_MP, RANK, n_tok)

    columns = lax.all_to_all(
        jnp.concatenate(
            [projected, jnp.broadcast_to(out_grad[None], (N_MP, n_tok, cols))], axis=1
        ),
        "mp",
        0,
        0,
        tiled=True,
    )
    partial_grad = local(
        subspace,
        bf16((N_MP, RANK, cols)),
        at,
        columns,
        ins=[VMEM],
        flops=2**25,
        moved=2**20,
        name="subspace",
    )

    theirs = lax.ppermute(partial_grad, "dp", SWAP)
    both = (partial_grad.astype(jnp.float32) + theirs.astype(jnp.float32)).astype(jnp.bfloat16)
    both, input_grad = lax.optimization_barrier((both, input_grad))
    input_grad = lax.psum_scatter(
        input_grad, "mp", scatter_dimension=0, axis_index_groups=GROUPS_Z, tiled=True
    )
    got = lax.all_to_all(both, "dp", 0, 0, axis_index_groups=ACROSS, tiled=True)

    packed_width = RANK // rows * first_moment.shape[1]
    new_first, new_second, packed = local(
        adam,
        (f32(first_moment.shape), f32(first_moment.shape), bf16((N_MP, rows, packed_width))),
        at,
        got,
        first_moment,
        second_moment,
        ins=[VMEM] * 3,
        flops=2**19,
        moved=2**20,
        name="adam",
    )
    update = local(
        back_project,
        bf16((first_moment.shape[1], width // N_MP)),
        at,
        mine,
        other,
        lax.all_to_all(packed, "mp", 0, 0, tiled=True),
        ins=[VMEM] * 3,
        flops=2 * 2**26,
        moved=2**21,
        name="back_project",
    )
    return (input_grad, update.T, new_first, new_second)


def solution(mesh):
    placed = (
        P(("dp", "mp"), None),
        P(None, "mp"),
        P("dp", "mp"),
        P(None, "mp"),
        P("mp", "dp"),
        P("mp", "dp"),
    )
    return jax.shard_map(
        body,
        mesh=mesh,
        in_specs=placed,
        out_specs=(P(("dp", "mp"), None), P("mp", "dp"), P("mp", "dp"), P("mp", "dp")),
        check_vma=False,
    )
```

time: 127 us -> 122 us (0.961)
  starting transfers between devices: 57.8 us -> 22.3 us
  blocking collectives: 24.6 us -> 59.3 us
  between operations: 0.89 us -> 14.2 us
  local copies, waits for them, and re-layouts: 8.15 us -> 0.21 us
  waiting for transfers between devices: 24.7 us -> 17.5 us
  Pallas kernels: 6.79 us -> 4.03 us
  matrix products: 0.58 us -> 2.64 us
    all_to_all x0 -> x2, blocking collectives: none -> 46.2 us  [the longest x1 25.2 us: body(): lax.all_to_all(jnp.concatenate([projected, jnp.broadcast_to(out_grad[None...]
    all_to_all x2 -> x0, starting transfers between devices: 19 us -> none  [the longest x1 11.9 us: body(): got = lax.all_to_all(both, 'dp', 0, 0, axis_index_groups=ACROSS, tiled=True)]
    ppermute x6 -> x0, starting transfers between devices: 18.8 us -> none  [the longest x3 11.3 us: along_x(): lax.ppermute(a, 'mp', [(m, (m + ZH * k) % N_MP) for m in range(N_MP)])]
    ppermute x6 -> x0, waiting for transfers between devices: 17.4 us -> none  [the longest x3 17.2 us: along_x(): lax.ppermute(a, 'mp', [(m, (m + ZH * k) % N_MP) for m in range(N_MP)])]
    all_to_all x1, waiting for transfers between devices: 0.01 us -> 14.9 us  [body(): mine = lax.all_to_all(packed, 'mp', 0, 0, tiled=True)]
    all_to_all x1, blocking collectives: 24.6 us -> 13.1 us  [body(): lax.all_to_all(packed, 'mp', 0, 0, tiled=True)]
    unnamed x22 -> x8, local copies, waits for them, and re-layouts: 5.01 us -> 0.03 us
    all_to_all x2 -> x0, waiting for transfers between devices: 4.86 us -> none  [the longest x1 2.62 us: body(): got = lax.all_to_all(both, 'dp', 0, 0, axis_index_groups=ACROSS, tiled=True)]
  transfers between devices with their start and end apart: 11 -> 5, of which waited for: 8 -> 3; matrix products, arithmetic and copies ran while one was open for 3% -> 3% of each run, Pallas kernels for 1% -> 2%
where the time goes in v3:
time: 122 us; the launch traced here: 121 us
  blocking collectives  59.3 us (49%)
  starting transfers between devices  22.3 us (18%)
  waiting for transfers between devices  17.5 us (14%)
  between operations  14.2 us (12%)
  Pallas kernels  4.03 us (3%)
  matrix products  2.64 us (2%)
    all_to_all x1, blocking collectives, body(): lax.all_to_all(jnp.concatenate([projected, jnp.broadcast_to(out_grad[None...  25.2 us
    all_to_all x1, blocking collectives, body(): got = lax.all_to_all(both, 'dp', 0, 0, axis_index_groups=ACROSS, tiled=True)  21.1 us
    all_to_all x1, waiting for transfers between devices, body(): mine = lax.all_to_all(packed, 'mp', 0, 0, tiled=True)  14.9 us
    all_to_all x1, starting transfers between devices, body(): mine = lax.all_to_all(packed, 'mp', 0, 0, tiled=True)  13.4 us
    all_to_all x1, blocking collectives, body(): lax.all_to_all(packed, 'mp', 0, 0, tiled=True)  13.1 us
    ppermute x1, starting transfers between devices, body(): theirs = lax.ppermute(partial_grad, 'dp', SWAP)  4.71 us
    ppermute x1, starting transfers between devices, body(): other = lax.ppermute(mine, 'dp', SWAP)  4.06 us
    pallas_call x4, Pallas kernels, local(): pl.pallas_call(kernel, out_shape=outs, in_specs=[pl.BlockSpec(memory_spac...  4.03 us
  transfers between devices with their start and end apart: 5, of which 3 were waited for; matrix products, arithmetic and copies ran while one was open for 3% of the time, Pallas kernels for 2%

profile of v3, /device:TPU:1, one launch (start us, length us, event | category | flops | bytes accessed | tf_op | source)
XLA Modules:
  0.0 121.0 jit_solution(1262447779259851529)
XLA Ops:
  7.2 0.0 copy-start
  7.2 0.0 copy-start.3
  7.2 2.1 %pack_rows.1 = bf16[16,80,256]{2,1,0:T(8,128)(2,1)} custom-call(s32[1]{0:T(128)} %bitcast.at_ref, bf16[64,8192]{1,0:T(8,128)(2,1)} %bitcast.18, bf16[8,8192]{1,0:T(8,128)(2,1)} %tok_ref.1), custom_call_target="tpu_custom_call" | custom-call | bytes 2097152 | tf_op jit(solution)/shard_map/pack_rows/pallas_call | solution.py:30
  9.3 13.4 %all-to-all-start = ((bf16[16,80,256]{2,1,0:T(8,128)(2,1)}), bf16[16,80,256]{2,1,0:T(8,128)(2,1)S(1)}, u32[]{:S(2)}, u32[]{:S(2)}) async-start(bf16[16,80,256]{2,1,0:T(8,128)(2,1)} %pack_rows.1), calls=%async_computation | async-start | bytes 1310720 | tf_op jit(solution)/shard_map/all_to_all | solution.py:140
  22.7 0.0 reduce-scatter.3.cloned.1.call-start
  22.8 0.0 copy-done
  22.8 0.0 copy-done.3
  22.8 2.1 %convolution_convert_fusion = bf16[128,8192]{1,0:T(8,128)(2,1)} fusion(bf16[128,128]{1,0:T(8,128)(2,1)S(1)} %copy-done.3, bf16[8192,128]{1,0:T(8,128)(2,1)S(1)} %copy-done), kind=kOutput, calls=%fused_computation | convolution fusion | flops 269484032 | bytes 4227072 | tf_op jit(solution)/shard_map/dot_general | solution.py:142
  24.8 0.0 reduce-scatter.3.cloned.1.call-update
  24.8 0.0 reduce-scatter.5.cloned.1.call-start
  24.9 14.9 %all-to-all-done.mine_ref = bf16[16,80,256]{2,1,0:T(8,128)(2,1)S(1)} async-done(((bf16[16,80,256]{2,1,0:T(8,128)(2,1)}), bf16[16,80,256]{2,1,0:T(8,128)(2,1)S(1)}, u32[]{:S(2)}, u32[]{:S(2)}) %all-to-all-start) | async-done | bytes 655392 | tf_op jit(solution)/shard_map/all_to_all | solution.py:140
  39.8 4.1 %collective-permute-start = (bf16[16,80,256]{2,1,0:T(8,128)(2,1)S(1)}, bf16[16,80,256]{2,1,0:T(8,128)(2,1)S(1)}, u32[]{:S(2)}, u32[]{:S(2)}) collective-permute-start(bf16[16,80,256]{2,1,0:T(8,128)(2,1)S(1)} %all-to-all-done.mine_ref), channel_id=1, source_target_pairs={{0,16},{16,0},{32,48},{48,32},{64,80},{80,64},{96,112},{112,96},{1... | collective-permute-start | bytes 1966088 | tf_op jit(solution)/shard_map/ppermute | solution.py:149
  44.0 0.3 fusion.1
  44.3 1.4 %collective-permute-done.other_ref = bf16[16,80,256]{2,1,0:T(8,128)(2,1)S(1)} collective-permute-done((bf16[16,80,256]{2,1,0:T(8,128)(2,1)S(1)}, bf16[16,80,256]{2,1,0:T(8,128)(2,1)S(1)}, u32[]{:S(2)}, u32[]{:S(2)}) %collective-permute-start) | collective-permute-done | bytes 655392 | tf_op jit(solution)/shard_map/ppermute | solution.py:149
  45.7 0.3 fusion
  46.0 0.1 broadcast_in_dim.10
  46.1 0.1 pad_maximum_fusion
  46.1 0.0 copy-start.1
  46.1 0.0 copy-start.2
  46.2 25.2 %all_to_all.20.got_ref = bf16[16,192,128]{2,1,0:T(8,128)(2,1)S(1)} all-to-all(bf16[16,192,128]{2,1,0:T(8,128)(2,1)S(1)} %pad_maximum_fusion), channel_id=1, replica_groups=mesh['dp'=32,'mp'=16] {'mp'}, dimensions={0} | all-to-all | bytes 1572864 | tf_op jit(solution)/shard_map/all_to_all | solution.py:164
  71.3 0.3 subspace.1
  71.6 4.7 %collective-permute-start.1 = (bf16[16,64,128]{2,1,0:T(8,128)(2,1)S(1)}, bf16[16,64,128]{2,1,0:T(8,128)(2,1)S(1)}, u32[]{:S(2)}, u32[]{:S(2)}) collective-permute-start(bf16[16,64,128]{2,1,0:T(8,128)(2,1)S(1)} %subspace.1), channel_id=1, source_target_pairs={{0,16},{16,0},{32,48},{48,32},{64,80},{80,64},{96,112},{112,96},{1... | collective-permute-start | bytes 786440 | tf_op jit(solution)/shard_map/ppermute | solution.py:184
  76.3 1.1 collective-permute-done.1
  77.5 0.8 add_convert_fusion
  78.2 0.0 reduce-scatter.3.cloned.1.call-done
  78.2 0.0 reduce-scatter.5.cloned.1.call-update
  78.3 21.1 %all_to_all.21.got_ref = bf16[16,64,128]{2,1,0:T(8,128)(2,1)S(1)} all-to-all(bf16[16,64,128]{2,1,0:T(8,128)(2,1)} %add_convert_fusion), channel_id=1, replica_groups={{0,32,64,96,128,160,192,224,256,288,320,352,384,416,448,480},{16,48,80,..., dimensions={0} | all-to-all | bytes 524288 | tf_op jit(solution)/shard_map/all_to_all | solution.py:190
  99.3 0.0 copy-done.1
  99.3 0.0 copy-done.2
  99.3 0.7 adam.1
  100.1 13.1 %all_to_all.22.got_ref = bf16[16,8,512]{2,1,0:T(8,128)(2,1)S(1)} all-to-all(bf16[16,8,512]{2,1,0:T(8,128)(2,1)S(1)} %get-tuple-element.17), channel_id=1, replica_groups=mesh['dp'=32,'mp'=16] {'mp'}, dimensions={0} | all-to-all | bytes 262144 | tf_op jit(solution)/shard_map/all_to_all | solution.py:211
  113.2 1.0 back_project.1
  114.1 0.0 reduce-scatter.5.cloned.1.call-done
  (2 shorter events, 0.1 us)
Async XLA Ops:
  7.2 15.6 %copy-start = (bf16[8192,128]{1,0:T(8,128)(2,1)S(1)}, bf16[8192,128]{1,0:T(8,128)(2,1)}, u32[]{:S(2)}) copy-start(bf16[8192,128]{1,0:T(8,128)(2,1)} %param.7) | copy-start | bytes 6291460
  7.2 15.6 %copy-start.3 = (bf16[128,128]{1,0:T(8,128)(2,1)S(1)}, bf16[128,128]{1,0:T(8,128)(2,1)}, u32[]{:S(2)}) copy-start(bf16[128,128]{1,0:T(8,128)(2,1)} %param.8) | copy-start | bytes 98308
  9.3 30.6 %all-to-all-start = ((bf16[16,80,256]{2,1,0:T(8,128)(2,1)}), bf16[16,80,256]{2,1,0:T(8,128)(2,1)S(1)}, u32[]{:S(2)}, u32[]{:S(2)}) async-start(bf16[16,80,256]{2,1,0:T(8,128)(2,1)} %pack_rows.1), calls=%async_computation | async-start | bytes 1310720 | tf_op jit(solution)/shard_map/all_to_all | solution.py:140
  22.7 55.5 %reduce-scatter.3.cloned.1.call-start = ((), (), s32[]{:S(2)}) async-start(), calls=%async_computation.6 | async-start | bytes 2621440 | tf_op jit(solution)/shard_map/reduce_scatter | solution.py:145
  24.8 89.3 %reduce-scatter.5.cloned.1.call-start = ((), (), s32[]{:S(2)}) async-start(), calls=%async_computation.7 | async-start | bytes 655360 | tf_op jit(solution)/shard_map/reduce_scatter | solution.py:187
  39.8 5.8 %collective-permute-start = (bf16[16,80,256]{2,1,0:T(8,128)(2,1)S(1)}, bf16[16,80,256]{2,1,0:T(8,128)(2,1)S(1)}, u32[]{:S(2)}, u32[]{:S(2)}) collective-permute-start(bf16[16,80,256]{2,1,0:T(8,128)(2,1)S(1)} %all-to-all-done.mine_ref), channel_id=1, source_target_pairs={{0,16},{16,0},{32,48},{48,32},{64,80},{80,64},{96,112},{112,96},{1... | collective-permute-start | bytes 1966088 | tf_op jit(solution)/shard_map/ppermute | solution.py:149
  46.1 53.2 %copy-start.1 = (f32[64,64]{1,0:T(8,128)S(1)}, f32[64,64]{1,0:T(8,128)}, u32[]{:S(2)}) copy-start(f32[64,64]{1,0:T(8,128)} %first_ref.1) | copy-start | bytes 49156
  46.1 53.2 %copy-start.2 = (f32[64,64]{1,0:T(8,128)S(1)}, f32[64,64]{1,0:T(8,128)}, u32[]{:S(2)}) copy-start(f32[64,64]{1,0:T(8,128)} %second_ref.1) | copy-start | bytes 49156
  71.6 5.9 %collective-permute-start.1 = (bf16[16,64,128]{2,1,0:T(8,128)(2,1)S(1)}, bf16[16,64,128]{2,1,0:T(8,128)(2,1)S(1)}, u32[]{:S(2)}, u32[]{:S(2)}) collective-permute-start(bf16[16,64,128]{2,1,0:T(8,128)(2,1)S(1)} %subspace.1), channel_id=1, source_target_pairs={{0,16},{16,0},{32,48},{48,32},{64,80},{80,64},{96,112},{112,96},{1... | collective-permute-start | bytes 786440 | tf_op jit(solution)/shard_map/ppermute | solution.py:184
Sparse Core Ops, SparseCore 0:
  26.4 44.3 reduce-scatter.2
  78.4 29.1 reduce-scatter.4

commit v4 on v3

--- a/solution.py
+++ b/solution.py
@@ -62,12 +62,11 @@
 
 
 def adam(at_ref, got_ref, first_ref, second_ref, new_first_ref, new_second_ref, out_ref):
-    core = at_ref[0]
     rank, width = first_ref.shape
     total = got_ref[0].astype(jnp.float32)
     for j in range(1, got_ref.shape[0]):
         total += got_ref[j].astype(jnp.float32)
-    grad = jnp.where(core == 0, total[:, :width], total[:, width:])
+    grad = jnp.concatenate([total[:, :width], total[:, width:]], axis=0)
     new_first = 0.9 * first_ref[...] + 0.1 * grad
     new_second = 0.999 * second_ref[...] + 0.001 * grad * grad
     new_first_ref[...] = new_first
@@ -104,15 +103,20 @@
         ).astype(update_ref.dtype)
 
 
-def subspace(at_ref, got_ref, out_ref):
+def subspace(at_ref, got_ref, mine_ref, other_ref):
+    core = at_ref[0]
     total = got_ref[0, :RANK, :].astype(jnp.float32)
     for j in range(1, N_MP):
         total += got_ref[j, :RANK, :].astype(jnp.float32)
     projected = total.astype(jnp.bfloat16)
     for j in range(N_MP):
-        out_ref[j] = jnp.dot(
-            projected, got_ref[j, RANK:, :], preferred_element_type=jnp.float32
-        ).astype(out_ref.dtype)
+        grad = jnp.dot(projected, got_ref[j, RANK:, :], preferred_element_type=jnp.float32)
+        width = grad.shape[1] // 2
+        low, high = grad[: RANK // 2], grad[RANK // 2 :]
+        first = jnp.concatenate([low[:, :width], high[:, :width]], axis=1)
+        second = jnp.concatenate([low[:, width:], high[:, width:]], axis=1)
+        mine_ref[j] = jnp.where(core == 0, first, second).astype(mine_ref.dtype)
+        other_ref[j] = jnp.where(core == 0, second, first).astype(other_ref.dtype)
 
 
 def body(tokens, kv_weight, out_grad, basis, first_moment, second_moment):
@@ -170,18 +174,18 @@
         0,
         tiled=True,
     )
-    partial_grad = local(
+    partial_grad, theirs = local(
         subspace,
-        bf16((N_MP, RANK, cols)),
+        (bf16((N_MP, RANK // 2, cols)), bf16((N_MP, RANK // 2, cols))),
         at,
         columns,
         ins=[VMEM],
-        flops=2**25,
+        flops=2**31,
         moved=2**20,
         name="subspace",
     )
 
-    theirs = lax.ppermute(partial_grad, "dp", SWAP)
+    theirs = lax.ppermute(theirs, "dp", SWAP)
     both = (partial_grad.astype(jnp.float32) + theirs.astype(jnp.float32)).astype(jnp.bfloat16)
     both, input_grad = lax.optimization_barrier((both, input_grad))
     input_grad = lax.psum_scatter(

time: 122 us -> 120 us (0.984)
  blocking collectives: 59.3 us -> 57.2 us
    all_to_all x1, blocking collectives: 21.1 us -> 18.5 us  [body(): got = lax.all_to_all(both, 'dp', 0, 0, axis_index_groups=ACROSS, tiled=True)]
where the time goes in v4:
time: 120 us; the launch traced here: 119 us
  blocking collectives  57.2 us (48%)
  starting transfers between devices  22.3 us (19%)
  waiting for transfers between devices  17.3 us (14%)
  between operations  14.2 us (12%)
  Pallas kernels  4.1 us (3%)
  matrix products  2.62 us (2%)
    all_to_all x1, blocking collectives, body(): lax.all_to_all(jnp.concatenate([projected, jnp.broadcast_to(out_grad[None...  25.2 us
    all_to_all x1, blocking collectives, body(): got = lax.all_to_all(both, 'dp', 0, 0, axis_index_groups=ACROSS, tiled=True)  18.5 us
    all_to_all x1, waiting for transfers between devices, body(): mine = lax.all_to_all(packed, 'mp', 0, 0, tiled=True)  14.9 us
    all_to_all x1, blocking collectives, body(): lax.all_to_all(packed, 'mp', 0, 0, tiled=True)  13.5 us
    all_to_all x1, starting transfers between devices, body(): mine = lax.all_to_all(packed, 'mp', 0, 0, tiled=True)  13.4 us
    ppermute x1, starting transfers between devices, body(): theirs = lax.ppermute(theirs, 'dp', SWAP)  4.72 us
    pallas_call x4, Pallas kernels, local(): pl.pallas_call(kernel, out_shape=outs, in_specs=[pl.BlockSpec(memory_spac...  4.1 us
    ppermute x1, starting transfers between devices, body(): other = lax.ppermute(mine, 'dp', SWAP)  4.06 us
  transfers between devices with their start and end apart: 5, of which 3 were waited for; matrix products, arithmetic and copies ran while one was open for 3% of the time, Pallas kernels for 2%

profile of v4, /device:TPU:1, one launch (start us, length us, event | category | flops | bytes accessed | tf_op | source)
XLA Modules:
  0.0 118.7 jit_solution(13363399181322129437)
XLA Ops:
  7.2 0.0 copy-start
  7.2 0.0 copy-start.3
  7.2 2.1 %pack_rows.1 = bf16[16,80,256]{2,1,0:T(8,128)(2,1)} custom-call(s32[1]{0:T(128)} %bitcast.at_ref, bf16[64,8192]{1,0:T(8,128)(2,1)} %bitcast.18, bf16[8,8192]{1,0:T(8,128)(2,1)} %tok_ref.1), custom_call_target="tpu_custom_call" | custom-call | bytes 2097152 | tf_op jit(solution)/shard_map/pack_rows/pallas_call | solution.py:30
  9.3 13.4 %all-to-all-start = ((bf16[16,80,256]{2,1,0:T(8,128)(2,1)}), bf16[16,80,256]{2,1,0:T(8,128)(2,1)S(1)}, u32[]{:S(2)}, u32[]{:S(2)}) async-start(bf16[16,80,256]{2,1,0:T(8,128)(2,1)} %pack_rows.1), calls=%async_computation | async-start | bytes 1310720 | tf_op jit(solution)/shard_map/all_to_all | solution.py:144
  22.7 0.0 reduce-scatter.3.cloned.1.call-start
  22.7 0.0 copy-done
  22.8 0.0 copy-done.3
  22.8 2.0 %convolution_convert_fusion = bf16[128,8192]{1,0:T(8,128)(2,1)} fusion(bf16[128,128]{1,0:T(8,128)(2,1)S(1)} %copy-done.3, bf16[8192,128]{1,0:T(8,128)(2,1)S(1)} %copy-done), kind=kOutput, calls=%fused_computation | convolution fusion | flops 269484032 | bytes 4227072 | tf_op jit(solution)/shard_map/dot_general | solution.py:146
  24.8 0.0 reduce-scatter.3.cloned.1.call-update
  24.8 0.0 reduce-scatter.5.cloned.1.call-start
  24.9 14.9 %all-to-all-done.mine_ref = bf16[16,80,256]{2,1,0:T(8,128)(2,1)S(1)} async-done(((bf16[16,80,256]{2,1,0:T(8,128)(2,1)}), bf16[16,80,256]{2,1,0:T(8,128)(2,1)S(1)}, u32[]{:S(2)}, u32[]{:S(2)}) %all-to-all-start) | async-done | bytes 655392 | tf_op jit(solution)/shard_map/all_to_all | solution.py:144
  39.8 4.1 %collective-permute-start = (bf16[16,80,256]{2,1,0:T(8,128)(2,1)S(1)}, bf16[16,80,256]{2,1,0:T(8,128)(2,1)S(1)}, u32[]{:S(2)}, u32[]{:S(2)}) collective-permute-start(bf16[16,80,256]{2,1,0:T(8,128)(2,1)S(1)} %all-to-all-done.mine_ref), channel_id=1, source_target_pairs={{0,16},{16,0},{32,48},{48,32},{64,80},{80,64},{96,112},{112,96},{1... | collective-permute-start | bytes 1966088 | tf_op jit(solution)/shard_map/ppermute | solution.py:153
  44.0 0.3 fusion.1
  44.2 1.4 %collective-permute-done.other_ref = bf16[16,80,256]{2,1,0:T(8,128)(2,1)S(1)} collective-permute-done((bf16[16,80,256]{2,1,0:T(8,128)(2,1)S(1)}, bf16[16,80,256]{2,1,0:T(8,128)(2,1)S(1)}, u32[]{:S(2)}, u32[]{:S(2)}) %collective-permute-start) | collective-permute-done | bytes 655392 | tf_op jit(solution)/shard_map/ppermute | solution.py:153
  45.7 0.3 fusion
  46.0 0.1 broadcast_in_dim.10
  46.1 0.1 pad_maximum_fusion
  46.1 25.2 %all_to_all.20.got_ref = bf16[16,192,128]{2,1,0:T(8,128)(2,1)S(1)} all-to-all(bf16[16,192,128]{2,1,0:T(8,128)(2,1)S(1)} %pad_maximum_fusion), channel_id=1, replica_groups=mesh['dp'=32,'mp'=16] {'mp'}, dimensions={0} | all-to-all | bytes 1572864 | tf_op jit(solution)/shard_map/all_to_all | solution.py:168
  71.3 0.0 copy-start.1
  71.3 0.0 copy-start.2
  71.3 0.4 subspace.1
  71.7 4.7 %collective-permute-start.1 = (bf16[16,32,128]{2,1,0:T(8,128)(2,1)S(1)}, bf16[16,32,128]{2,1,0:T(8,128)(2,1)S(1)}, u32[]{:S(2)}, u32[]{:S(2)}) collective-permute-start(bf16[16,32,128]{2,1,0:T(8,128)(2,1)S(1)} %get-tuple-element.17), channel_id=1, source_target_pairs={{0,16},{16,0},{32,48},{48,32},{64,80},{80,64},{96,112},{112,96},{1... | collective-permute-start | bytes 393224 | tf_op jit(solution)/shard_map/ppermute | solution.py:188
  76.4 1.0 collective-permute-done.1
  77.4 0.7 add_convert_fusion
  78.1 0.0 reduce-scatter.3.cloned.1.call-done
  78.1 0.0 reduce-scatter.5.cloned.1.call-update
  78.1 18.5 %all_to_all.21.got_ref = bf16[16,32,128]{2,1,0:T(8,128)(2,1)S(1)} all-to-all(bf16[16,32,128]{2,1,0:T(8,128)(2,1)} %add_convert_fusion), channel_id=1, replica_groups={{0,32,64,96,128,160,192,224,256,288,320,352,384,416,448,480},{16,48,80,..., dimensions={0} | all-to-all | bytes 262144 | tf_op jit(solution)/shard_map/all_to_all | solution.py:194
  96.6 0.0 copy-done.1
  96.6 0.0 copy-done.2
  96.6 0.7 adam.1
  97.3 13.5 %all_to_all.22.got_ref = bf16[16,8,512]{2,1,0:T(8,128)(2,1)S(1)} all-to-all(bf16[16,8,512]{2,1,0:T(8,128)(2,1)S(1)} %get-tuple-element.21), channel_id=1, replica_groups=mesh['dp'=32,'mp'=16] {'mp'}, dimensions={0} | all-to-all | bytes 262144 | tf_op jit(solution)/shard_map/all_to_all | solution.py:215
  110.9 1.0 back_project.1
  111.8 0.0 reduce-scatter.5.cloned.1.call-done
  (2 shorter events, 0.1 us)
Async XLA Ops:
  7.2 15.6 %copy-start = (bf16[8192,128]{1,0:T(8,128)(2,1)S(1)}, bf16[8192,128]{1,0:T(8,128)(2,1)}, u32[]{:S(2)}) copy-start(bf16[8192,128]{1,0:T(8,128)(2,1)} %param.7) | copy-start | bytes 6291460
  7.2 15.6 %copy-start.3 = (bf16[128,128]{1,0:T(8,128)(2,1)S(1)}, bf16[128,128]{1,0:T(8,128)(2,1)}, u32[]{:S(2)}) copy-start(bf16[128,128]{1,0:T(8,128)(2,1)} %param.8) | copy-start | bytes 98308
  9.3 30.6 %all-to-all-start = ((bf16[16,80,256]{2,1,0:T(8,128)(2,1)}), bf16[16,80,256]{2,1,0:T(8,128)(2,1)S(1)}, u32[]{:S(2)}, u32[]{:S(2)}) async-start(bf16[16,80,256]{2,1,0:T(8,128)(2,1)} %pack_rows.1), calls=%async_computation | async-start | bytes 1310720 | tf_op jit(solution)/shard_map/all_to_all | solution.py:144
  22.7 55.4 %reduce-scatter.3.cloned.1.call-start = ((), (), s32[]{:S(2)}) async-start(), calls=%async_computation.6 | async-start | bytes 2621440 | tf_op jit(solution)/shard_map/reduce_scatter | solution.py:149
  24.8 87.0 %reduce-scatter.5.cloned.1.call-start = ((), (), s32[]{:S(2)}) async-start(), calls=%async_computation.7 | async-start | bytes 655360 | tf_op jit(solution)/shard_map/reduce_scatter | solution.py:191
  39.8 5.8 %collective-permute-start = (bf16[16,80,256]{2,1,0:T(8,128)(2,1)S(1)}, bf16[16,80,256]{2,1,0:T(8,128)(2,1)S(1)}, u32[]{:S(2)}, u32[]{:S(2)}) collective-permute-start(bf16[16,80,256]{2,1,0:T(8,128)(2,1)S(1)} %all-to-all-done.mine_ref), channel_id=1, source_target_pairs={{0,16},{16,0},{32,48},{48,32},{64,80},{80,64},{96,112},{112,96},{1... | collective-permute-start | bytes 1966088 | tf_op jit(solution)/shard_map/ppermute | solution.py:153
  71.3 25.3 %copy-start.1 = (f32[64,64]{1,0:T(8,128)S(1)}, f32[64,64]{1,0:T(8,128)}, u32[]{:S(2)}) copy-start(f32[64,64]{1,0:T(8,128)} %first_ref.1) | copy-start | bytes 49156
  71.3 25.3 %copy-start.2 = (f32[64,64]{1,0:T(8,128)S(1)}, f32[64,64]{1,0:T(8,128)}, u32[]{:S(2)}) copy-start(f32[64,64]{1,0:T(8,128)} %second_ref.1) | copy-start | bytes 49156
  71.7 5.7 %collective-permute-start.1 = (bf16[16,32,128]{2,1,0:T(8,128)(2,1)S(1)}, bf16[16,32,128]{2,1,0:T(8,128)(2,1)S(1)}, u32[]{:S(2)}, u32[]{:S(2)}) collective-permute-start(bf16[16,32,128]{2,1,0:T(8,128)(2,1)S(1)} %get-tuple-element.17), channel_id=1, source_target_pairs={{0,16},{16,0},{32,48},{48,32},{64,80},{80,64},{96,112},{112,96},{1... | collective-permute-start | bytes 393224 | tf_op jit(solution)/shard_map/ppermute | solution.py:188
Sparse Core Ops, SparseCore 0:
  26.4 44.4 reduce-scatter.2
  78.2 28.7 reduce-scatter.4

commit v5 on v4

--- a/solution.py
+++ b/solution.py
@@ -19,7 +19,7 @@
 SWAP = [(d, d ^ 1) for d in range(N_DP)]
 NT = (((1,), (1,)), ((), ()))
 TN = (((0,), (0,)), ((), ()))
-LIMIT = 48 * 2**20
+LIMIT = 16 * 2**20
 
 
 VMEM = pl.BlockSpec(memory_space=pltpu.VMEM)
@@ -61,14 +61,20 @@
         copy.wait()
 
 
-def adam(at_ref, got_ref, first_ref, second_ref, new_first_ref, new_second_ref, out_ref):
-    rank, width = first_ref.shape
+def combine(at_ref, mine_ref, theirs_ref, out_ref):
+    out_ref[...] = (mine_ref[...].astype(jnp.float32) + theirs_ref[...].astype(jnp.float32)).astype(
+        out_ref.dtype
+    )
+
+
+def adam(at_ref, got_ref, parts_ref, new_first_ref, new_second_ref, out_ref):
+    rank, width = parts_ref.shape[1:]
     total = got_ref[0].astype(jnp.float32)
     for j in range(1, got_ref.shape[0]):
         total += got_ref[j].astype(jnp.float32)
     grad = jnp.concatenate([total[:, :width], total[:, width:]], axis=0)
-    new_first = 0.9 * first_ref[...] + 0.1 * grad
-    new_second = 0.999 * second_ref[...] + 0.001 * grad * grad
+    new_first = parts_ref[0] + 0.1 * grad
+    new_second = parts_ref[1] + 0.001 * grad * grad
     new_first_ref[...] = new_first
     new_second_ref[...] = new_second
     first_scale = 1.0 - 0.9**STEP
@@ -180,13 +186,29 @@
         at,
         columns,
         ins=[VMEM],
-        flops=2**31,
+        flops=2**32,
         moved=2**20,
         name="subspace",
     )
 
+    partial_grad, theirs, first_moment, second_moment = lax.optimization_barrier(
+        (partial_grad, theirs, first_moment, second_moment)
+    )
     theirs = lax.ppermute(theirs, "dp", SWAP)
-    both = (partial_grad.astype(jnp.float32) + theirs.astype(jnp.float32)).astype(jnp.bfloat16)
+
+    parts = jnp.stack([0.9 * first_moment, 0.999 * second_moment])
+    theirs, parts = lax.optimization_barrier((theirs, parts))
+    both = local(
+        combine,
+        bf16(partial_grad.shape),
+        at,
+        partial_grad,
+        theirs,
+        ins=[VMEM] * 2,
+        flops=2**16,
+        moved=2**18,
+        name="combine",
+    )
     both, input_grad = lax.optimization_barrier((both, input_grad))
     input_grad = lax.psum_scatter(
         input_grad, "mp", scatter_dimension=0, axis_index_groups=GROUPS_Z, tiled=True
@@ -199,9 +221,8 @@
         (f32(first_moment.shape), f32(first_moment.shape), bf16((N_MP, rows, packed_width))),
         at,
         got,
-        first_moment,
-        second_moment,
-        ins=[VMEM] * 3,
+        parts,
+        ins=[VMEM] * 2,
         flops=2**19,
         moved=2**20,
         name="adam",

time: 120 us -> 120 us (level)
    pallas_call x4 -> x5, Pallas kernels: 4.1 us -> 4.12 us  [local(): pl.pallas_call(kernel, out_shape=outs, in_specs=[pl.BlockSpec(memory_spac...]
where the time goes in v5:
time: 120 us; the launch traced here: 118 us
  blocking collectives  56.6 us (47%)
  starting transfers between devices  22.3 us (19%)
  waiting for transfers between devices  16.6 us (14%)
  between operations  14.2 us (12%)
  Pallas kernels  4.12 us (3%)
  matrix products  2.64 us (2%)
    all_to_all x1, blocking collectives, body(): lax.all_to_all(jnp.concatenate([projected, jnp.broadcast_to(out_grad[None...  25.2 us
    all_to_all x1, blocking collectives, body(): got = lax.all_to_all(both, 'dp', 0, 0, axis_index_groups=ACROSS, tiled=True)  18.3 us
    all_to_all x1, waiting for transfers between devices, body(): mine = lax.all_to_all(packed, 'mp', 0, 0, tiled=True)  14.9 us
    all_to_all x1, starting transfers between devices, body(): mine = lax.all_to_all(packed, 'mp', 0, 0, tiled=True)  13.4 us
    all_to_all x1, blocking collectives, body(): lax.all_to_all(packed, 'mp', 0, 0, tiled=True)  13.1 us
    ppermute x1, starting transfers between devices, body(): theirs = lax.ppermute(theirs, 'dp', SWAP)  4.71 us
    pallas_call x5, Pallas kernels, local(): pl.pallas_call(kernel, out_shape=outs, in_specs=[pl.BlockSpec(memory_spac...  4.12 us
    ppermute x1, starting transfers between devices, body(): other = lax.ppermute(mine, 'dp', SWAP)  4.06 us
  transfers between devices with their start and end apart: 5, of which 3 were waited for; matrix products, arithmetic and copies ran while one was open for 3% of the time, Pallas kernels for 2%

profile of v5, /device:TPU:1, one launch (start us, length us, event | category | flops | bytes accessed | tf_op | source)
XLA Modules:
  0.0 118.2 jit_solution(16744914743428809720)
XLA Ops:
  7.2 0.0 copy-start
  7.2 0.0 copy-start.2
  7.2 2.0 %pack_rows.1 = bf16[16,80,256]{2,1,0:T(8,128)(2,1)} custom-call(s32[1]{0:T(128)} %bitcast.at_ref, bf16[64,8192]{1,0:T(8,128)(2,1)} %bitcast.22, bf16[8,8192]{1,0:T(8,128)(2,1)} %tok_ref.1), custom_call_target="tpu_custom_call" | custom-call | bytes 2097152 | tf_op jit(solution)/shard_map/pack_rows/pallas_call | solution.py:30
  9.3 13.4 %all-to-all-start = ((bf16[16,80,256]{2,1,0:T(8,128)(2,1)}), bf16[16,80,256]{2,1,0:T(8,128)(2,1)S(1)}, u32[]{:S(2)}, u32[]{:S(2)}) async-start(bf16[16,80,256]{2,1,0:T(8,128)(2,1)} %pack_rows.1), calls=%async_computation | async-start | bytes 1310720 | tf_op jit(solution)/shard_map/all_to_all | solution.py:150
  22.7 0.0 reduce-scatter.3.cloned.1.call-start
  22.7 0.0 copy-done
  22.8 0.0 copy-done.2
  22.8 2.0 %convolution_convert_fusion = bf16[128,8192]{1,0:T(8,128)(2,1)} fusion(bf16[128,128]{1,0:T(8,128)(2,1)S(1)} %copy-done.2, bf16[8192,128]{1,0:T(8,128)(2,1)S(1)} %copy-done), kind=kOutput, calls=%fused_computation | convolution fusion | flops 269484032 | bytes 4227072 | tf_op jit(solution)/shard_map/dot_general | solution.py:152
  24.8 0.0 reduce-scatter.3.cloned.1.call-update
  24.8 0.0 reduce-scatter.5.cloned.1.call-start
  24.9 14.9 %all-to-all-done.mine_ref = bf16[16,80,256]{2,1,0:T(8,128)(2,1)S(1)} async-done(((bf16[16,80,256]{2,1,0:T(8,128)(2,1)}), bf16[16,80,256]{2,1,0:T(8,128)(2,1)S(1)}, u32[]{:S(2)}, u32[]{:S(2)}) %all-to-all-start) | async-done | bytes 655392 | tf_op jit(solution)/shard_map/all_to_all | solution.py:150
  39.8 4.1 %collective-permute-start = (bf16[16,80,256]{2,1,0:T(8,128)(2,1)S(1)}, bf16[16,80,256]{2,1,0:T(8,128)(2,1)S(1)}, u32[]{:S(2)}, u32[]{:S(2)}) collective-permute-start(bf16[16,80,256]{2,1,0:T(8,128)(2,1)S(1)} %all-to-all-done.mine_ref), channel_id=1, source_target_pairs={{0,16},{16,0},{32,48},{48,32},{64,80},{80,64},{96,112},{112,96},{1... | collective-permute-start | bytes 1966088 | tf_op jit(solution)/shard_map/ppermute | solution.py:159
  44.0 0.3 fusion.1
  44.3 1.3 %collective-permute-done.other_ref = bf16[16,80,256]{2,1,0:T(8,128)(2,1)S(1)} collective-permute-done((bf16[16,80,256]{2,1,0:T(8,128)(2,1)S(1)}, bf16[16,80,256]{2,1,0:T(8,128)(2,1)S(1)}, u32[]{:S(2)}, u32[]{:S(2)}) %collective-permute-start) | collective-permute-done | bytes 655392 | tf_op jit(solution)/shard_map/ppermute | solution.py:159
  45.7 0.3 fusion
  46.0 0.1 broadcast_in_dim.10
  46.1 0.1 pad_maximum_fusion
  46.1 25.2 %all_to_all.20.got_ref = bf16[16,192,128]{2,1,0:T(8,128)(2,1)S(1)} all-to-all(bf16[16,192,128]{2,1,0:T(8,128)(2,1)S(1)} %pad_maximum_fusion), channel_id=1, replica_groups=mesh['dp'=32,'mp'=16] {'mp'}, dimensions={0} | all-to-all | bytes 1572864 | tf_op jit(solution)/shard_map/all_to_all | solution.py:174
  71.3 0.0 copy-start.3
  71.3 0.0 copy-start.4
  71.3 0.4 subspace.1
  71.7 4.7 %collective-permute-start.1 = (bf16[16,32,128]{2,1,0:T(8,128)(2,1)S(1)}, bf16[16,32,128]{2,1,0:T(8,128)(2,1)S(1)}, u32[]{:S(2)}, u32[]{:S(2)}) collective-permute-start(bf16[16,32,128]{2,1,0:T(8,128)(2,1)S(1)} %get-tuple-element.25), channel_id=1, source_target_pairs={{0,16},{16,0},{32,48},{48,32},{64,80},{80,64},{96,112},{112,96},{1... | collective-permute-start | bytes 393224 | tf_op jit(solution)/shard_map/ppermute | solution.py:197
  76.4 0.0 copy-done.3
  76.4 0.0 copy-done.4
  76.4 0.6 pad_maximum_fusion.1.parts_ref
  77.1 0.3 collective-permute-done.1.theirs_ref
  77.4 0.0 reduce-scatter.3.cloned.1.call-done
  77.4 0.0 reduce-scatter.5.cloned.1.call-update
  77.4 18.3 %all_to_all.21.got_ref = bf16[16,32,128]{2,1,0:T(8,128)(2,1)S(1)} all-to-all(bf16[16,32,128]{2,1,0:T(8,128)(2,1)S(1)} %combine.1), channel_id=1, replica_groups={{0,32,64,96,128,160,192,224,256,288,320,352,384,416,448,480},{16,48,80,..., dimensions={0} | all-to-all | bytes 262144 | tf_op jit(solution)/shard_map/all_to_all | solution.py:216
  95.8 0.0 copy-start.1
  95.8 0.8 copy-done.1
  96.6 0.7 adam.1
  97.3 13.1 %all_to_all.22.got_ref = bf16[16,8,512]{2,1,0:T(8,128)(2,1)S(1)} all-to-all(bf16[16,8,512]{2,1,0:T(8,128)(2,1)S(1)} %get-tuple-element.33), channel_id=1, replica_groups=mesh['dp'=32,'mp'=16] {'mp'}, dimensions={0} | all-to-all | bytes 262144 | tf_op jit(solution)/shard_map/all_to_all | solution.py:236
  110.4 1.0 back_project.1
  111.4 0.0 reduce-scatter.5.cloned.1.call-done
  (4 shorter events, 0.1 us)
Async XLA Ops:
  7.2 15.6 %copy-start = (bf16[8192,128]{1,0:T(8,128)(2,1)S(1)}, bf16[8192,128]{1,0:T(8,128)(2,1)}, u32[]{:S(2)}) copy-start(bf16[8192,128]{1,0:T(8,128)(2,1)} %param.7) | copy-start | bytes 6291460
  7.2 15.6 %copy-start.2 = (bf16[128,128]{1,0:T(8,128)(2,1)S(1)}, bf16[128,128]{1,0:T(8,128)(2,1)}, u32[]{:S(2)}) copy-start(bf16[128,128]{1,0:T(8,128)(2,1)} %param.8) | copy-start | bytes 98308
  9.3 30.6 %all-to-all-start = ((bf16[16,80,256]{2,1,0:T(8,128)(2,1)}), bf16[16,80,256]{2,1,0:T(8,128)(2,1)S(1)}, u32[]{:S(2)}, u32[]{:S(2)}) async-start(bf16[16,80,256]{2,1,0:T(8,128)(2,1)} %pack_rows.1), calls=%async_computation | async-start | bytes 1310720 | tf_op jit(solution)/shard_map/all_to_all | solution.py:150
  22.7 54.7 %reduce-scatter.3.cloned.1.call-start = ((), (), s32[]{:S(2)}) async-start(), calls=%async_computation.6 | async-start | bytes 2621440 | tf_op jit(solution)/shard_map/reduce_scatter | solution.py:155
  24.8 86.6 %reduce-scatter.5.cloned.1.call-start = ((), (), s32[]{:S(2)}) async-start(), calls=%async_computation.7 | async-start | bytes 655360 | tf_op jit(solution)/shard_map/reduce_scatter | solution.py:213
  39.8 5.8 %collective-permute-start = (bf16[16,80,256]{2,1,0:T(8,128)(2,1)S(1)}, bf16[16,80,256]{2,1,0:T(8,128)(2,1)S(1)}, u32[]{:S(2)}, u32[]{:S(2)}) collective-permute-start(bf16[16,80,256]{2,1,0:T(8,128)(2,1)S(1)} %all-to-all-done.mine_ref), channel_id=1, source_target_pairs={{0,16},{16,0},{32,48},{48,32},{64,80},{80,64},{96,112},{112,96},{1... | collective-permute-start | bytes 1966088 | tf_op jit(solution)/shard_map/ppermute | solution.py:159
  71.3 5.1 %copy-start.3 = (f32[64,64]{1,0:T(8,128)S(1)}, f32[64,64]{1,0:T(8,128)}, u32[]{:S(2)}) copy-start(f32[64,64]{1,0:T(8,128)} %param.11) | copy-start | bytes 49156
  71.3 5.1 %copy-start.4 = (f32[64,64]{1,0:T(8,128)S(1)}, f32[64,64]{1,0:T(8,128)}, u32[]{:S(2)}) copy-start(f32[64,64]{1,0:T(8,128)} %param.10) | copy-start | bytes 49156
  71.7 5.7 %collective-permute-start.1 = (bf16[16,32,128]{2,1,0:T(8,128)(2,1)S(1)}, bf16[16,32,128]{2,1,0:T(8,128)(2,1)S(1)}, u32[]{:S(2)}, u32[]{:S(2)}) collective-permute-start(bf16[16,32,128]{2,1,0:T(8,128)(2,1)S(1)} %get-tuple-element.25), channel_id=1, source_target_pairs={{0,16},{16,0},{32,48},{48,32},{64,80},{80,64},{96,112},{112,96},{1... | collective-permute-start | bytes 393224 | tf_op jit(solution)/shard_map/ppermute | solution.py:197
  95.8 0.8 copy-start.1
Sparse Core Ops, SparseCore 0:
  26.4 44.4 reduce-scatter.2
  77.6 27.7 reduce-scatter.4
